TPU v7x, 32 devices: a whole 2x2x4 slice. The times are simulated.
32 devices in a mesh: lon: 8 (over z, y), band: 4 (over x, core).
Axes of the slice: x: 2, y: 2, z: 4, core: 2. Of those that a mesh axis runs over, the one named last changes fastest.
Arguments:
- denoised_tokens: bfloat16 [4, 32, 1920], P('band', 'lon'), may hold values from -6 to 6
- sequence_row_index: int32 [4, 32], P('band'), may hold values from 0 to 31, each once within a row
- latent_frame_cache: bfloat16 [4, 128, 1920], P(None, 'band', 'lon'), may hold values from -6 to 6
- cache_slot_order: int32 [4], replicated, may hold values from 0 to 3, each once
- temporal_taps_weight: bfloat16 [3, 16, 16], replicated, may hold values from -0.875 to 0.875
- input_weight: bfloat16 [9, 16, 256], replicated, may hold values from -0.5 to 0.5
- latent_conv_weights: bfloat16 [2, 9, 256, 256], replicated, may hold values from -0.125 to 0.125
- upsampled_weight: bfloat16 [9, 256, 256], replicated, may hold values from -0.125 to 0.125
- upper_conv_weights: bfloat16 [2, 9, 256, 256], replicated, may hold values from -0.125 to 0.125
- latent_norm_gains: float32 [2, 256], replicated, may hold values from 0.5 to 1.5
- upper_norm_gains: float32 [2, 256], replicated, may hold values from 0.5 to 1.5
Outputs:
- decoded: bfloat16 [256, 240, 256], P('band', 'lon')
Inputs may be any that keep to these rules, and one draw needn't show every extreme that they name: Each row sequence_row_index[b] holds every position 0..31 once. cache_slot_order holds each slot once.
All inputs are finite; a program needn't handle non-finite values.
Results may differ from a plain program's by a relative error of at most 0.02.
Values may be sent and summed in bfloat16 or wider, within the bound.
A program may use at most 128 MiB of HBM per device.

v0:
```python
import jax
import jax.numpy as jnp
from jax import lax
from jax.sharding import PartitionSpec as P


def padded_2(block, sides, width, periodic):
    for axis, dim in sides:
        count = lax.axis_size(axis)
        forward = [(i, i + 1) for i in range(count - 1)]
        if periodic:
            forward.append((count - 1, 0))
        backward = [(target, source) for source, target in forward]
        low = lax.ppermute(
            lax.slice_in_dim(block, block.shape[dim] - width, None, axis=dim), axis, forward
        )
        high = lax.ppermute(lax.slice_in_dim(block, 0, width, axis=dim), axis, backward)
        block = jnp.concatenate([low, block, high], axis=dim)
    return block


def activate(activity, gain_row):
    values = activity.astype(jnp.float32)
    scaled = (
        values * lax.rsqrt(jnp.mean(values * values, axis=-1, keepdims=True) + 1e-06) * gain_row
    )
    return jax.nn.silu(scaled).astype(jnp.bfloat16)


def conv_valid(padded, weight):
    row_count = padded.shape[0] - 2
    col_count = padded.shape[1] - 2
    inputs = padded.shape[2]
    summed = jnp.zeros((row_count * col_count, weight.shape[2]), jnp.float32)
    for offset in range(9):
        shift_row = offset // 3
        shift_col = offset % 3
        window = padded[
            shift_row : shift_row + row_count, shift_col : shift_col + col_count
        ].reshape(row_count * col_count, inputs)
        summed = summed + jnp.dot(window, weight[offset], preferred_element_type=jnp.float32)
    return summed.reshape(row_count, col_count, weight.shape[2])


def with_rims(activity):
    widened = padded_2(activity, (("lon", 1),), 1, True)
    return padded_2(widened, (("band", 0),), 1, False)


def upsample(activity):
    return jnp.repeat(jnp.repeat(activity, 2, axis=0), 2, axis=1)


def block_single(activity, gain_rows, weights):
    inner_sum = conv_valid(with_rims(activate(activity, gain_rows[0])), weights[0])
    branch = conv_valid(with_rims(activate(inner_sum, gain_rows[1])), weights[1])
    return (activity.astype(jnp.float32) + branch).astype(jnp.bfloat16)


def run_block(activity, gain_rows, weights):
    return block_single(activity, gain_rows, weights)


def shards(
    denoised_tokens,
    sequence_row_index,
    latent_frame_cache,
    cache_slot_order,
    temporal_taps_weight,
    input_weight,
    latent_conv_weights,
    upsampled_weight,
    upper_conv_weights,
    latent_norm_gains,
    upper_norm_gains,
):
    token_sequence = denoised_tokens.reshape(denoised_tokens.shape[1], denoised_tokens.shape[2])
    arrived = lax.all_to_all(token_sequence, "lon", split_axis=1, concat_axis=0, tiled=True)
    band_rows = arrived.shape[0]
    channels = temporal_taps_weight.shape[1]
    sector_cols = arrived.shape[1] // channels
    latent = arrived[sequence_row_index[0]].reshape(band_rows * sector_cols, channels)
    newest = latent_frame_cache[cache_slot_order[0]].reshape(band_rows * sector_cols, channels)
    oldest = latent_frame_cache[cache_slot_order[1]].reshape(band_rows * sector_cols, channels)
    mixture = jnp.dot(latent, temporal_taps_weight[0], preferred_element_type=jnp.float32)
    mixture = mixture + jnp.dot(newest, temporal_taps_weight[1], preferred_element_type=jnp.float32)
    mixture = mixture + jnp.dot(oldest, temporal_taps_weight[2], preferred_element_type=jnp.float32)
    temporal = mixture.astype(jnp.bfloat16).reshape(band_rows, sector_cols, channels)
    opening = conv_valid(with_rims(temporal), input_weight).astype(jnp.bfloat16)
    low_res = run_block(opening, latent_norm_gains, latent_conv_weights)
    padded = with_rims(upsample(low_res))
    high_res = conv_valid(padded, upsampled_weight).astype(jnp.bfloat16)
    return run_block(high_res, upper_norm_gains, upper_conv_weights)


def solution(mesh):
    in_specs = (
        P("band", "lon", None),
        P("band", None),
        P(None, "band", "lon"),
        P(),
        P(),
        P(),
        P(),
        P(),
        P(),
        P(),
        P(),
    )
    out_specs = P("band", "lon", None)
    return jax.shard_map(shards, mesh=mesh, in_specs=in_specs, out_specs=out_specs, check_vma=False)
```

profile of v0, /device:TPU:1, one launch (start us, length us, event | category | flops | bytes accessed | tf_op | source)
XLA Modules:
  0.0 265.3 jit_solution(6039824589882468054)
XLA Ops:
  1.5 6.4 %all-to-all-start = ((bf16[4,8,240]{2,0,1:T(4,128)(2,1)}), bf16[4,8,240]{2,0,1:T(4,128)(2,1)S(1)}, u32[]{:S(2)}, u32[]{:S(2)}) async-start(bf16[4,8,240]{2,0,1:T(4,128)(2,1)} %copy.38), calls=%async_computation | async-start | bytes 32768 | tf_op jit(solution)/shard_map/all_to_all | solution.py:78
  20.9 2.8 %collective-permute-start.1 = (bf16[32,1,16]{1,0,2:T(8,128)(2,1)S(1)}, bf16[32,1,16]{1,0,2:T(8,128)(2,1)S(1)}, u32[]{:S(2)}, u32[]{:S(2)}) collective-permute-start(bf16[32,1,16]{1,0,2:T(8,128)(2,1)S(1)} %get-tuple-element.86), channel_id=1, source_target_pairs={{4,0},{8,4},{12,8},{16,12},{20,16},{24,20},{28,24},{0,28},{5,1},{9... | collective-permute-start | bytes 3080 | tf_op jit(solution)/shard_map/ppermute | solution.py:17
  23.9 2.1 collective-permute-done
  26.0 1.6 collective-permute-done.1
  27.8 5.0 %collective-permute-start.2 = (bf16[1,17,16]{1,0,2:T(2,128)(2,1)S(1)}, bf16[1,17,16]{1,0,2:T(2,128)(2,1)S(1)}, u32[]{:S(2)}, u32[]{:S(2)}) collective-permute-start(bf16[1,17,16]{1,0,2:T(2,128)(2,1)S(1)} %get-tuple-element.83), channel_id=1, source_target_pairs={{0,1},{1,2},{2,3},{4,5},{5,6},{6,7},{8,9},{9,10},{10,11},{12,13},{... | collective-permute-start | bytes 1640 | tf_op jit(solution)/shard_map/ppermute | solution.py:14
  32.8 1.9 collective-permute-start.3
  35.5 2.3 collective-permute-done.3
  44.0 3.9 %collective-permute-start.5 = (bf16[32,1,256]{2,1,0:T(2,128)(2,1)S(1)}, bf16[32,1,256]{2,1,0:T(2,128)(2,1)S(1)}, u32[]{:S(2)}, u32[]{:S(2)}) collective-permute-start(bf16[32,1,256]{2,1,0:T(2,128)(2,1)S(1)} %get-tuple-element.74), channel_id=1, source_target_pairs={{4,0},{8,4},{12,8},{16,12},{20,16},{24,20},{28,24},{0,28},{5,1},{9... | collective-permute-start | bytes 49160 | tf_op jit(solution)/shard_map/ppermute | solution.py:17
  47.9 2.0 fusion.17
  49.9 2.5 collective-permute-start.6
  52.4 1.9 collective-permute-start.7
  54.8 2.6 collective-permute-done.7
  68.9 3.9 %collective-permute-start.9 = (bf16[32,1,256]{2,1,0:T(2,128)(2,1)S(1)}, bf16[32,1,256]{2,1,0:T(2,128)(2,1)S(1)}, u32[]{:S(2)}, u32[]{:S(2)}) collective-permute-start(bf16[32,1,256]{2,1,0:T(2,128)(2,1)S(1)} %get-tuple-element.70), channel_id=1, source_target_pairs={{4,0},{8,4},{12,8},{16,12},{20,16},{24,20},{28,24},{0,28},{5,1},{9... | collective-permute-start | bytes 49160 | tf_op jit(solution)/shard_map/ppermute | solution.py:17
  72.8 2.0 fusion.18
  74.9 2.3 collective-permute-start.10
  77.2 13.8 %collective-permute-start.11 = (bf16[1,17,256]{2,1,0:T(8,128)(2,1)S(1)}, bf16[1,17,256]{2,1,0:T(8,128)(2,1)S(1)}, u32[]{:S(2)}, u32[]{:S(2)}) collective-permute-start(bf16[1,17,256]{2,1,0:T(8,128)(2,1)S(1)} %get-tuple-element.62), channel_id=1, source_target_pairs={{1,0},{2,1},{3,2},{5,4},{6,5},{7,6},{9,8},{10,9},{11,10},{13,12},{... | collective-permute-start | bytes 26120 | tf_op jit(solution)/shard_map/ppermute | solution.py:17
  102.9 4.3 %collective-permute-start.13 = (bf16[64,1,256]{2,0,1:T(8,128)(2,1)S(1)}, bf16[64,1,256]{2,0,1:T(8,128)(2,1)S(1)}, u32[]{:S(2)}, u32[]{:S(2)}) collective-permute-start(bf16[64,1,256]{2,0,1:T(8,128)(2,1)S(1)} %get-tuple-element.46), channel_id=1, source_target_pairs={{4,0},{8,4},{12,8},{16,12},{20,16},{24,20},{28,24},{0,28},{5,1},{9... | collective-permute-start | bytes 98312 | tf_op jit(solution)/shard_map/ppermute | solution.py:17
  109.4 1.9 collective-permute-start.15
  111.4 4.0 %collective-permute-start.14 = (bf16[1,32,256]{2,0,1:T(2,128)(2,1)S(1)}, bf16[1,32,256]{2,0,1:T(2,128)(2,1)S(1)}, u32[]{:S(2)}, u32[]{:S(2)}) collective-permute-start(bf16[1,32,256]{2,0,1:T(2,128)(2,1)S(1)} %get-tuple-element.42), channel_id=1, source_target_pairs={{0,1},{1,2},{2,3},{4,5},{5,6},{6,7},{8,9},{9,10},{10,11},{12,13},{... | collective-permute-start | bytes 49160 | tf_op jit(solution)/shard_map/ppermute | solution.py:14
  119.9 1.6 fusion.151
  123.2 1.8 copy.57
  130.8 1.8 copy.50
  133.8 1.7 fusion.49
  143.2 1.7 multiply_reduce_fusion.1
  145.0 2.0 reshape.422
  147.9 4.2 %collective-permute-start.17 = (bf16[64,1,256]{2,1,0:T(2,128)(2,1)S(1)}, bf16[64,1,256]{2,1,0:T(2,128)(2,1)S(1)}, u32[]{:S(2)}, u32[]{:S(2)}) collective-permute-start(bf16[64,1,256]{2,1,0:T(2,128)(2,1)S(1)} %get-tuple-element.38), channel_id=1, source_target_pairs={{4,0},{8,4},{12,8},{16,12},{20,16},{24,20},{28,24},{0,28},{5,1},{9... | collective-permute-start | bytes 98312 | tf_op jit(solution)/shard_map/ppermute | solution.py:17
  152.1 2.9 %fusion.15 = f32[1920,256]{1,0:T(8,128)} fusion(f32[1920,256]{1,0:T(8,128)S(1)} %copy-done.3, f32[256]{0:T(256)S(1)} %bitcast.276, f32[1920]{0:T(1024)S(1)} %add_rsqrt_fusion.1, bf16[2,9,256,256]{3,2,1,0:T(8,128)(2,1)} %param.19), kind=kOutput, calls=%fused_computation.75 | convolution fusion | flops 255098880 | bytes 4071936 | tf_op jit(solution)/shard_map/dot_general | solution.py:41
  155.0 2.9 %collective-permute-start.18 = (bf16[1,32,256]{2,1,0:T(8,128)(2,1)S(1)}, bf16[1,32,256]{2,1,0:T(8,128)(2,1)S(1)}, u32[]{:S(2)}, u32[]{:S(2)}) collective-permute-start(bf16[1,32,256]{2,1,0:T(8,128)(2,1)S(1)} %get-tuple-element.11), channel_id=1, source_target_pairs={{0,1},{1,2},{2,3},{4,5},{5,6},{6,7},{8,9},{9,10},{10,11},{12,13},{... | collective-permute-start | bytes 49160 | tf_op jit(solution)/shard_map/ppermute | solution.py:14
  157.9 1.9 collective-permute-start.19
  159.9 2.5 pad_maximum_fusion.5
  162.4 2.2 reshape.407
  164.6 2.2 reshape.406
  166.8 1.9 maximum_maximum_fusion.1
  168.7 2.1 fusion.156
  170.8 2.2 reshape.405
  174.2 3.0 %fusion.38 = f32[1920,256]{1,0:T(8,128)} fusion(bf16[1920,256]{1,0:T(8,128)(2,1)} %reshape.404, bf16[2,9,256,256]{3,2,1,0:T(8,128)(2,1)} %param.19), kind=kOutput, calls=%fused_computation.116 | convolution fusion | flops 251658240 | bytes 3080192 | tf_op jit(solution)/shard_map/dot_general | solution.py:41
  177.2 2.2 reshape.403
  179.3 2.6 fusion.155
  181.9 2.3 reshape.410
  184.2 2.2 reshape.409
  187.6 1.8 fusion.32
  194.5 1.5 fusion.2
  197.5 2.6 multiply_reduce_fusion
  200.3 2.7 %reshape.411 = f32[64,30,256]{2,1,0:T(8,128)} reshape(f32[1920,256]{1,0:T(8,128)} %get-tuple-element.105) | data formatting | bytes 3932160 | tf_op jit(solution)/shard_map/reshape | solution.py:42
  203.0 2.3 multiply_convert_fusion
  205.5 4.1 %collective-permute-start.21 = (bf16[64,1,256]{2,1,0:T(2,128)(2,1)S(1)}, bf16[64,1,256]{2,1,0:T(2,128)(2,1)S(1)}, u32[]{:S(2)}, u32[]{:S(2)}) collective-permute-start(bf16[64,1,256]{2,1,0:T(2,128)(2,1)S(1)} %get-tuple-element.34), channel_id=1, source_target_pairs={{4,0},{8,4},{12,8},{16,12},{20,16},{24,20},{28,24},{0,28},{5,1},{9... | collective-permute-start | bytes 98312 | tf_op jit(solution)/shard_map/ppermute | solution.py:17
  209.7 2.9 %fusion.16 = f32[1920,256]{1,0:T(8,128)} fusion(f32[1920,256]{1,0:T(8,128)S(1)} %copy-done.2, f32[256]{0:T(256)S(1)} %bitcast.272, f32[1920]{0:T(1024)S(1)} %add_rsqrt_fusion, bf16[2,9,256,256]{3,2,1,0:T(8,128)(2,1)} %param.19), kind=kOutput, calls=%fused_computation.76 | convolution fusion | flops 255098880 | bytes 4071936 | tf_op jit(solution)/shard_map/dot_general | solution.py:41
  212.6 4.2 %collective-permute-start.22 = (bf16[1,32,256]{2,1,0:T(8,128)(2,1)S(1)}, bf16[1,32,256]{2,1,0:T(8,128)(2,1)S(1)}, u32[]{:S(2)}, u32[]{:S(2)}) collective-permute-start(bf16[1,32,256]{2,1,0:T(8,128)(2,1)S(1)} %get-tuple-element.7), channel_id=1, source_target_pairs={{0,1},{1,2},{2,3},{4,5},{5,6},{6,7},{8,9},{9,10},{10,11},{12,13},{... | collective-permute-start | bytes 49160 | tf_op jit(solution)/shard_map/ppermute | solution.py:14
  216.8 1.9 collective-permute-start.23
  218.7 2.5 pad_maximum_fusion.3
  221.3 2.4 reshape.416
  223.7 2.2 reshape.415
  225.8 1.9 maximum_maximum_fusion.2
  227.7 2.1 fusion.154
  229.8 2.2 reshape.414
  233.2 3.0 %fusion.27 = f32[1920,256]{1,0:T(8,128)} fusion(bf16[1920,256]{1,0:T(8,128)(2,1)} %reshape.413, bf16[2,9,256,256]{3,2,1,0:T(8,128)(2,1)} %param.19), kind=kOutput, calls=%fused_computation.105 | convolution fusion | flops 251658240 | bytes 3080192 | tf_op jit(solution)/shard_map/dot_general | solution.py:41
  236.2 2.2 reshape.412
  238.4 2.6 fusion.153
  240.9 2.3 reshape.419
  243.2 2.2 reshape.418
  246.6 1.8 fusion.21
  256.4 2.6 convolution_add_fusion
  259.0 2.7 %reshape.420 = f32[64,30,256]{2,1,0:T(8,128)} reshape(f32[1920,256]{1,0:T(8,128)} %convolution_add_fusion) | data formatting | bytes 3932160 | tf_op jit(solution)/shard_map/reshape | solution.py:42
  261.7 1.9 add_convert_fusion
  (250 shorter events, 86.6 us)
Async XLA Ops:
  0.0 23.6 %copy-start.31 = (bf16[9,16,256]{2,1,0:T(8,128)(2,1)S(1)}, bf16[9,16,256]{2,1,0:T(8,128)(2,1)}, u32[]{:S(2)}) copy-start(bf16[9,16,256]{2,1,0:T(8,128)(2,1)} %param.16) | copy-start | bytes 221188
  1.5 14.0 %all-to-all-start = ((bf16[4,8,240]{2,0,1:T(4,128)(2,1)}), bf16[4,8,240]{2,0,1:T(4,128)(2,1)S(1)}, u32[]{:S(2)}, u32[]{:S(2)}) async-start(bf16[4,8,240]{2,0,1:T(4,128)(2,1)} %copy.38), calls=%async_computation | async-start | bytes 32768 | tf_op jit(solution)/shard_map/all_to_all | solution.py:78
  19.3 6.7 %collective-permute-start = (bf16[32,1,16]{1,0,2:T(8,128)(2,1)S(1)}, bf16[32,1,16]{1,0,2:T(8,128)(2,1)S(1)}, u32[]{:S(2)}, u32[]{:S(2)}) collective-permute-start(bf16[32,1,16]{1,0,2:T(8,128)(2,1)S(1)} %get-tuple-element.85), channel_id=1, source_target_pairs={{0,4},{4,8},{8,12},{12,16},{16,20},{20,24},{24,28},{28,0},{1,5},{5... | collective-permute-start | bytes 3080 | tf_op jit(solution)/shard_map/ppermute | solution.py:14
  20.9 6.8 %collective-permute-start.1 = (bf16[32,1,16]{1,0,2:T(8,128)(2,1)S(1)}, bf16[32,1,16]{1,0,2:T(8,128)(2,1)S(1)}, u32[]{:S(2)}, u32[]{:S(2)}) collective-permute-start(bf16[32,1,16]{1,0,2:T(8,128)(2,1)S(1)} %get-tuple-element.86), channel_id=1, source_target_pairs={{4,0},{8,4},{12,8},{16,12},{20,16},{24,20},{28,24},{0,28},{5,1},{9... | collective-permute-start | bytes 3080 | tf_op jit(solution)/shard_map/ppermute | solution.py:17
  27.8 10.2 %collective-permute-start.2 = (bf16[1,17,16]{1,0,2:T(2,128)(2,1)S(1)}, bf16[1,17,16]{1,0,2:T(2,128)(2,1)S(1)}, u32[]{:S(2)}, u32[]{:S(2)}) collective-permute-start(bf16[1,17,16]{1,0,2:T(2,128)(2,1)S(1)} %get-tuple-element.83), channel_id=1, source_target_pairs={{0,1},{1,2},{2,3},{4,5},{5,6},{6,7},{8,9},{9,10},{10,11},{12,13},{... | collective-permute-start | bytes 1640 | tf_op jit(solution)/shard_map/ppermute | solution.py:14
  32.8 5.0 %collective-permute-start.3 = (bf16[1,17,16]{1,0,2:T(2,128)(2,1)S(1)}, bf16[1,17,16]{1,0,2:T(2,128)(2,1)S(1)}, u32[]{:S(2)}, u32[]{:S(2)}) collective-permute-start(bf16[1,17,16]{1,0,2:T(2,128)(2,1)S(1)} %get-tuple-element.84), channel_id=1, source_target_pairs={{1,0},{2,1},{3,2},{5,4},{6,5},{7,6},{9,8},{10,9},{11,10},{13,12},{... | collective-permute-start | bytes 1640 | tf_op jit(solution)/shard_map/ppermute | solution.py:17
  43.6 6.2 %collective-permute-start.4 = (bf16[32,1,256]{2,1,0:T(2,128)(2,1)S(1)}, bf16[32,1,256]{2,1,0:T(2,128)(2,1)S(1)}, u32[]{:S(2)}, u32[]{:S(2)}) collective-permute-start(bf16[32,1,256]{2,1,0:T(2,128)(2,1)S(1)} %get-tuple-element.73), channel_id=1, source_target_pairs={{0,4},{4,8},{8,12},{12,16},{16,20},{20,24},{24,28},{28,0},{1,5},{5... | collective-permute-start | bytes 49160 | tf_op jit(solution)/shard_map/ppermute | solution.py:14
  44.0 5.9 %collective-permute-start.5 = (bf16[32,1,256]{2,1,0:T(2,128)(2,1)S(1)}, bf16[32,1,256]{2,1,0:T(2,128)(2,1)S(1)}, u32[]{:S(2)}, u32[]{:S(2)}) collective-permute-start(bf16[32,1,256]{2,1,0:T(2,128)(2,1)S(1)} %get-tuple-element.74), channel_id=1, source_target_pairs={{4,0},{8,4},{12,8},{16,12},{20,16},{24,20},{28,24},{0,28},{5,1},{9... | collective-permute-start | bytes 49160 | tf_op jit(solution)/shard_map/ppermute | solution.py:17
  49.9 4.9 %collective-permute-start.6 = (bf16[1,17,256]{2,1,0:T(8,128)(2,1)S(1)}, bf16[1,17,256]{2,1,0:T(8,128)(2,1)S(1)}, u32[]{:S(2)}, u32[]{:S(2)}) collective-permute-start(bf16[1,17,256]{2,1,0:T(8,128)(2,1)S(1)} %get-tuple-element.65), channel_id=1, source_target_pairs={{0,1},{1,2},{2,3},{4,5},{5,6},{6,7},{8,9},{9,10},{10,11},{12,13},{... | collective-permute-start | bytes 26120 | tf_op jit(solution)/shard_map/ppermute | solution.py:14
  52.4 5.0 %collective-permute-start.7 = (bf16[1,17,256]{2,1,0:T(8,128)(2,1)S(1)}, bf16[1,17,256]{2,1,0:T(8,128)(2,1)S(1)}, u32[]{:S(2)}, u32[]{:S(2)}) collective-permute-start(bf16[1,17,256]{2,1,0:T(8,128)(2,1)S(1)} %get-tuple-element.66), channel_id=1, source_target_pairs={{1,0},{2,1},{3,2},{5,4},{6,5},{7,6},{9,8},{10,9},{11,10},{13,12},{... | collective-permute-start | bytes 26120 | tf_op jit(solution)/shard_map/ppermute | solution.py:17
  60.9 2.3 copy-start.30
  68.4 6.4 %collective-permute-start.8 = (bf16[32,1,256]{2,1,0:T(2,128)(2,1)S(1)}, bf16[32,1,256]{2,1,0:T(2,128)(2,1)S(1)}, u32[]{:S(2)}, u32[]{:S(2)}) collective-permute-start(bf16[32,1,256]{2,1,0:T(2,128)(2,1)S(1)} %get-tuple-element.69), channel_id=1, source_target_pairs={{0,4},{4,8},{8,12},{12,16},{16,20},{20,24},{24,28},{28,0},{1,5},{5... | collective-permute-start | bytes 49160 | tf_op jit(solution)/shard_map/ppermute | solution.py:14
  68.9 6.0 %collective-permute-start.9 = (bf16[32,1,256]{2,1,0:T(2,128)(2,1)S(1)}, bf16[32,1,256]{2,1,0:T(2,128)(2,1)S(1)}, u32[]{:S(2)}, u32[]{:S(2)}) collective-permute-start(bf16[32,1,256]{2,1,0:T(2,128)(2,1)S(1)} %get-tuple-element.70), channel_id=1, source_target_pairs={{4,0},{8,4},{12,8},{16,12},{20,16},{24,20},{28,24},{0,28},{5,1},{9... | collective-permute-start | bytes 49160 | tf_op jit(solution)/shard_map/ppermute | solution.py:17
  74.9 16.6 %collective-permute-start.10 = (bf16[1,17,256]{2,1,0:T(8,128)(2,1)S(1)}, bf16[1,17,256]{2,1,0:T(8,128)(2,1)S(1)}, u32[]{:S(2)}, u32[]{:S(2)}) collective-permute-start(bf16[1,17,256]{2,1,0:T(8,128)(2,1)S(1)} %get-tuple-element.61), channel_id=1, source_target_pairs={{0,1},{1,2},{2,3},{4,5},{5,6},{6,7},{8,9},{9,10},{10,11},{12,13},{... | collective-permute-start | bytes 26120 | tf_op jit(solution)/shard_map/ppermute | solution.py:14
  77.2 14.3 %collective-permute-start.11 = (bf16[1,17,256]{2,1,0:T(8,128)(2,1)S(1)}, bf16[1,17,256]{2,1,0:T(8,128)(2,1)S(1)}, u32[]{:S(2)}, u32[]{:S(2)}) collective-permute-start(bf16[1,17,256]{2,1,0:T(8,128)(2,1)S(1)} %get-tuple-element.62), channel_id=1, source_target_pairs={{1,0},{2,1},{3,2},{5,4},{6,5},{7,6},{9,8},{10,9},{11,10},{13,12},{... | collective-permute-start | bytes 26120 | tf_op jit(solution)/shard_map/ppermute | solution.py:17
  93.8 3.5 %copy-start.29 = (f32[480,256]{1,0:T(8,128)S(1)}, f32[480,256]{1,0:T(8,128)}, u32[]{:S(2)}) copy-start(f32[480,256]{1,0:T(8,128)} %fusion.18) | copy-start | bytes 1474564
  102.0 5.1 %copy-start.32 = (f32[2,256]{1,0:T(2,128)S(1)}, f32[2,256]{1,0:T(2,128)}, u32[]{:S(2)}) copy-start(f32[2,256]{1,0:T(2,128)} %param.21) | copy-start | bytes 6148
  102.8 6.5 %collective-permute-start.12 = (bf16[64,1,256]{2,0,1:T(8,128)(2,1)S(1)}, bf16[64,1,256]{2,0,1:T(8,128)(2,1)S(1)}, u32[]{:S(2)}, u32[]{:S(2)}) collective-permute-start(bf16[64,1,256]{2,0,1:T(8,128)(2,1)S(1)} %get-tuple-element.45), channel_id=1, source_target_pairs={{0,4},{4,8},{8,12},{12,16},{16,20},{20,24},{24,28},{28,0},{1,5},{5... | collective-permute-start | bytes 98312 | tf_op jit(solution)/shard_map/ppermute | solution.py:14
  102.9 6.5 %collective-permute-start.13 = (bf16[64,1,256]{2,0,1:T(8,128)(2,1)S(1)}, bf16[64,1,256]{2,0,1:T(8,128)(2,1)S(1)}, u32[]{:S(2)}, u32[]{:S(2)}) collective-permute-start(bf16[64,1,256]{2,0,1:T(8,128)(2,1)S(1)} %get-tuple-element.46), channel_id=1, source_target_pairs={{4,0},{8,4},{12,8},{16,12},{20,16},{24,20},{28,24},{0,28},{5,1},{9... | collective-permute-start | bytes 98312 | tf_op jit(solution)/shard_map/ppermute | solution.py:17
  109.4 9.7 %collective-permute-start.15 = (bf16[1,32,256]{2,0,1:T(2,128)(2,1)S(1)}, bf16[1,32,256]{2,0,1:T(2,128)(2,1)S(1)}, u32[]{:S(2)}, u32[]{:S(2)}) collective-permute-start(bf16[1,32,256]{2,0,1:T(2,128)(2,1)S(1)} %get-tuple-element.41), channel_id=1, source_target_pairs={{1,0},{2,1},{3,2},{5,4},{6,5},{7,6},{9,8},{10,9},{11,10},{13,12},{... | collective-permute-start | bytes 49160 | tf_op jit(solution)/shard_map/ppermute | solution.py:17
  111.4 7.7 %collective-permute-start.14 = (bf16[1,32,256]{2,0,1:T(2,128)(2,1)S(1)}, bf16[1,32,256]{2,0,1:T(2,128)(2,1)S(1)}, u32[]{:S(2)}, u32[]{:S(2)}) collective-permute-start(bf16[1,32,256]{2,0,1:T(2,128)(2,1)S(1)} %get-tuple-element.42), channel_id=1, source_target_pairs={{0,1},{1,2},{2,3},{4,5},{5,6},{6,7},{8,9},{9,10},{10,11},{12,13},{... | collective-permute-start | bytes 49160 | tf_op jit(solution)/shard_map/ppermute | solution.py:14
  133.8 1.7 copy-start.28
  135.9 1.2 copy-start.10
  137.2 1.2 copy-start.8
  138.4 1.2 copy-start.9
  139.6 1.2 copy-start.13
  140.8 1.2 copy-start.12
  142.0 1.2 copy-start.11
  147.0 5.0 %copy-start.3 = (f32[1920,256]{1,0:T(8,128)S(1)}, f32[1920,256]{1,0:T(8,128)}, u32[]{:S(2)}) copy-start(f32[1920,256]{1,0:T(8,128)} %get-tuple-element.103) | copy-start | bytes 5898244
  147.8 7.2 %collective-permute-start.16 = (bf16[64,1,256]{2,1,0:T(2,128)(2,1)S(1)}, bf16[64,1,256]{2,1,0:T(2,128)(2,1)S(1)}, u32[]{:S(2)}, u32[]{:S(2)}) collective-permute-start(bf16[64,1,256]{2,1,0:T(2,128)(2,1)S(1)} %get-tuple-element.37), channel_id=1, source_target_pairs={{0,4},{4,8},{8,12},{12,16},{16,20},{20,24},{24,28},{28,0},{1,5},{5... | collective-permute-start | bytes 98312 | tf_op jit(solution)/shard_map/ppermute | solution.py:14
  147.9 7.1 %collective-permute-start.17 = (bf16[64,1,256]{2,1,0:T(2,128)(2,1)S(1)}, bf16[64,1,256]{2,1,0:T(2,128)(2,1)S(1)}, u32[]{:S(2)}, u32[]{:S(2)}) collective-permute-start(bf16[64,1,256]{2,1,0:T(2,128)(2,1)S(1)} %get-tuple-element.38), channel_id=1, source_target_pairs={{4,0},{8,4},{12,8},{16,12},{20,16},{24,20},{28,24},{0,28},{5,1},{9... | collective-permute-start | bytes 98312 | tf_op jit(solution)/shard_map/ppermute | solution.py:17
  155.0 11.8 %collective-permute-start.18 = (bf16[1,32,256]{2,1,0:T(8,128)(2,1)S(1)}, bf16[1,32,256]{2,1,0:T(8,128)(2,1)S(1)}, u32[]{:S(2)}, u32[]{:S(2)}) collective-permute-start(bf16[1,32,256]{2,1,0:T(8,128)(2,1)S(1)} %get-tuple-element.11), channel_id=1, source_target_pairs={{0,1},{1,2},{2,3},{4,5},{5,6},{6,7},{8,9},{9,10},{10,11},{12,13},{... | collective-permute-start | bytes 49160 | tf_op jit(solution)/shard_map/ppermute | solution.py:14
  157.9 8.9 %collective-permute-start.19 = (bf16[1,32,256]{2,1,0:T(8,128)(2,1)S(1)}, bf16[1,32,256]{2,1,0:T(8,128)(2,1)S(1)}, u32[]{:S(2)}, u32[]{:S(2)}) collective-permute-start(bf16[1,32,256]{2,1,0:T(8,128)(2,1)S(1)} %get-tuple-element.12), channel_id=1, source_target_pairs={{1,0},{2,1},{3,2},{5,4},{6,5},{7,6},{9,8},{10,9},{11,10},{13,12},{... | collective-permute-start | bytes 49160 | tf_op jit(solution)/shard_map/ppermute | solution.py:17
  174.2 5.2 %copy-start = (bf16[65,32,256]{2,1,0:T(8,128)(2,1)S(1)}, bf16[65,32,256]{2,1,0:T(8,128)(2,1)}, u32[]{:S(2)}) copy-start(bf16[65,32,256]{2,1,0:T(8,128)(2,1)} %get-tuple-element.10) | copy-start | bytes 3194884
  181.9 4.5 %copy-start.6 = (bf16[64,30,256]{2,1,0:T(8,128)(2,1)S(1)}, bf16[64,30,256]{2,1,0:T(8,128)(2,1)}, u32[]{:S(2)}) copy-start(bf16[64,30,256]{2,1,0:T(8,128)(2,1)} %get-tuple-element.27) | copy-start | bytes 2949124
  187.6 1.9 copy-start.4
  187.6 2.1 copy-start.20
  189.7 1.4 copy-start.15
  191.2 1.5 copy-start.24
  191.2 1.9 copy-start.26
  193.1 1.4 copy-start.22
  194.5 1.6 copy-start.18
  196.1 1.4 copy-start.14
  203.0 6.7 %copy-start.2 = (f32[1920,256]{1,0:T(8,128)S(1)}, f32[1920,256]{1,0:T(8,128)}, u32[]{:S(2)}) copy-start(f32[1920,256]{1,0:T(8,128)} %get-tuple-element.105) | copy-start | bytes 5898244
  205.4 7.1 %collective-permute-start.20 = (bf16[64,1,256]{2,1,0:T(2,128)(2,1)S(1)}, bf16[64,1,256]{2,1,0:T(2,128)(2,1)S(1)}, u32[]{:S(2)}, u32[]{:S(2)}) collective-permute-start(bf16[64,1,256]{2,1,0:T(2,128)(2,1)S(1)} %get-tuple-element.33), channel_id=1, source_target_pairs={{0,4},{4,8},{8,12},{12,16},{16,20},{20,24},{24,28},{28,0},{1,5},{5... | collective-permute-start | bytes 98312 | tf_op jit(solution)/shard_map/ppermute | solution.py:14
  205.5 7.1 %collective-permute-start.21 = (bf16[64,1,256]{2,1,0:T(2,128)(2,1)S(1)}, bf16[64,1,256]{2,1,0:T(2,128)(2,1)S(1)}, u32[]{:S(2)}, u32[]{:S(2)}) collective-permute-start(bf16[64,1,256]{2,1,0:T(2,128)(2,1)S(1)} %get-tuple-element.34), channel_id=1, source_target_pairs={{4,0},{8,4},{12,8},{16,12},{20,16},{24,20},{28,24},{0,28},{5,1},{9... | collective-permute-start | bytes 98312 | tf_op jit(solution)/shard_map/ppermute | solution.py:17
  212.6 13.2 %collective-permute-start.22 = (bf16[1,32,256]{2,1,0:T(8,128)(2,1)S(1)}, bf16[1,32,256]{2,1,0:T(8,128)(2,1)S(1)}, u32[]{:S(2)}, u32[]{:S(2)}) collective-permute-start(bf16[1,32,256]{2,1,0:T(8,128)(2,1)S(1)} %get-tuple-element.7), channel_id=1, source_target_pairs={{0,1},{1,2},{2,3},{4,5},{5,6},{6,7},{8,9},{9,10},{10,11},{12,13},{... | collective-permute-start | bytes 49160 | tf_op jit(solution)/shard_map/ppermute | solution.py:14
  216.8 9.0 %collective-permute-start.23 = (bf16[1,32,256]{2,1,0:T(8,128)(2,1)S(1)}, bf16[1,32,256]{2,1,0:T(8,128)(2,1)S(1)}, u32[]{:S(2)}, u32[]{:S(2)}) collective-permute-start(bf16[1,32,256]{2,1,0:T(8,128)(2,1)S(1)} %get-tuple-element.8), channel_id=1, source_target_pairs={{1,0},{2,1},{3,2},{5,4},{6,5},{7,6},{9,8},{10,9},{11,10},{13,12},{... | collective-permute-start | bytes 49160 | tf_op jit(solution)/shard_map/ppermute | solution.py:17
  233.2 5.2 %copy-start.1 = (bf16[65,32,256]{2,1,0:T(8,128)(2,1)S(1)}, bf16[65,32,256]{2,1,0:T(8,128)(2,1)}, u32[]{:S(2)}) copy-start(bf16[65,32,256]{2,1,0:T(8,128)(2,1)} %get-tuple-element.6) | copy-start | bytes 3194884
  240.9 4.5 %copy-start.7 = (bf16[64,30,256]{2,1,0:T(8,128)(2,1)S(1)}, bf16[64,30,256]{2,1,0:T(8,128)(2,1)}, u32[]{:S(2)}) copy-start(bf16[64,30,256]{2,1,0:T(8,128)(2,1)} %get-tuple-element.21) | copy-start | bytes 2949124
  246.6 1.9 copy-start.5
  246.6 2.1 copy-start.21
  248.8 1.4 copy-start.16
  250.2 1.5 copy-start.25
  250.2 1.9 copy-start.27
  252.1 1.4 copy-start.23
  253.5 1.4 copy-start.19
  255.0 1.4 copy-start.17
where the time goes:
time: 270 us; the launch traced here: 265 us
  local copies, waits for them, and re-layouts  88.8 us (33%)
  starting transfers between devices  76.4 us (28%)
  matrix products  68.6 us (25%)
  other arithmetic  17.7 us (7%)
  waiting for transfers between devices  8.69 us (3%)
  between operations  5.15 us (2%)
    dot_general x54, matrix products, conv_valid(): jnp.dot(window, weight[offset], preferred_element_type=jnp.float32)  66 us
    ppermute x12, starting transfers between devices, padded_2(): lax.ppermute(lax.slice_in_dim(block, 0, width, axis=dim), axis, backward)  46.6 us
    reshape x48, local copies, waits for them, and re-layouts, conv_valid(): window = padded[shift_row:shift_row + row_count, shift_col:shift_col + co...  42.4 us
    ppermute x12, starting transfers between devices, padded_2(): lax.ppermute(lax.slice_in_dim(block, block.shape[dim] - width, None, axis...  23.4 us
    slice x23, local copies, waits for them, and re-layouts, conv_valid(): padded[shift_row:shift_row + row_count, shift_col:shift_col + col_count]  20.8 us
    concatenate x14, other arithmetic, padded_2(): block = jnp.concatenate([low, block, high], axis=dim)  11.4 us
    unnamed x67, local copies, waits for them, and re-layouts  6.57 us
    ppermute x12, waiting for transfers between devices, padded_2(): lax.ppermute(lax.slice_in_dim(block, 0, width, axis=dim), axis, backward)  6.54 us
  transfers between devices with their start and end apart: 25, of which 4 were waited for; matrix products, arithmetic and copies ran while one was open for 13% of the time, Pallas kernels for 0%

commit v1 on v0

v1 whole, which is shorter than its diff:
```python
import functools

import jax
import jax.numpy as jnp
from jax import lax
from jax.experimental import pallas as pl
from jax.experimental.pallas import tpu as pltpu
from jax.sharding import PartitionSpec as P

HALO = 5
F32 = jnp.float32
BF16 = jnp.bfloat16


def round_up(value, step):
    return (value + step - 1) // step * step


def tile_of(rows, pitch, even=False):
    best = 2 if even else 1
    for count in range(1, rows + 1):
        if rows % count == 0 and count * pitch <= 640 and not (even and count % 2):
            best = count
    return best


def activate(values, gain):
    scale = lax.rsqrt(jnp.mean(values * values, axis=-1, keepdims=True) + 1e-06)
    half = values * scale * (gain * 0.5)
    return half + half * jnp.tanh(half)


def roll_up(values, count):
    return pltpu.roll(values, values.shape[0] - count, 0)


def decoder_kernel(
    dims,
    band_ref,
    patches_ref,
    first_ref,
    low_w_ref,
    up_w_ref,
    high_w_ref,
    low_gain_ref,
    high_gain_ref,
    out_ref,
    opening,
    low_a,
    low_b,
    low_res,
    phase_w,
    field,
    high_a,
    high_b,
    weave,
):
    rows, cols, pitch, narrow, bands = dims
    ch = out_ref.shape[-1]
    band = band_ref[0]
    at_top = band == 0
    at_bottom = band == bands - 1

    def blank(ref, lead, row_slice):
        shape = ref.at[lead, row_slice].shape if lead is not None else ref.at[row_slice].shape
        if lead is None:
            ref[row_slice] = jnp.zeros(shape, ref.dtype)
        else:
            ref[lead, row_slice] = jnp.zeros(shape, ref.dtype)

    def blank_ends(ref, copies, top, bottom):
        total = ref.shape[1]

        @pl.when(at_top)
        def _():
            for k in range(copies):
                blank(ref, k, pl.ds(0, top))

        @pl.when(at_bottom)
        def _():
            for k in range(copies):
                blank(ref, k, pl.ds(total - bottom, bottom))

    total = rows + 8
    tile = tile_of(total, pitch)

    @pl.loop(0, total // tile)
    def _(step):
        start = step * tile
        part = patches_ref[pl.ds(start, tile)].reshape(tile * pitch, -1)
        summed = jnp.dot(part, first_ref[...], preferred_element_type=F32)
        summed = summed.astype(BF16).astype(F32)
        shape = (tile, pitch, ch)
        opening[pl.ds(start, tile)] = roll_up(summed, 2).astype(BF16).reshape(shape)
        active = activate(summed, low_gain_ref[0:1])
        low_a[0, pl.ds(start, tile)] = active.astype(BF16).reshape(shape)
        low_a[1, pl.ds(start, tile)] = roll_up(active, 1).astype(BF16).reshape(shape)
        low_a[2, pl.ds(start, tile)] = roll_up(active, 2).astype(BF16).reshape(shape)

    blank_ends(low_a, 3, 4, 4)

    def low_conv(source, start, tile, which):
        parts = []
        for p in range(3):
            for q in range(3):
                part = source[q, pl.ds(start + p, tile)]
                parts.append(part.reshape(tile * pitch, ch))
        return jnp.dot(
            jnp.concatenate(parts, axis=1), low_w_ref[which], preferred_element_type=F32
        )

    total = rows + 6
    tile = tile_of(total, pitch)

    @pl.loop(0, total // tile)
    def _(step):
        start = step * tile
        shape = (tile, pitch, ch)
        active = activate(low_conv(low_a, start, tile, 0), low_gain_ref[1:2])
        low_b[0, pl.ds(start, tile)] = active.astype(BF16).reshape(shape)
        low_b[1, pl.ds(start, tile)] = roll_up(active, 1).astype(BF16).reshape(shape)
        low_b[2, pl.ds(start, tile)] = roll_up(active, 2).astype(BF16).reshape(shape)

    blank_ends(low_b, 3, 3, 3)

    total = rows + 4
    tile = tile_of(total, pitch)

    @pl.loop(0, total // tile)
    def _(step):
        start = step * tile
        shape = (tile, pitch, ch)
        summed = low_conv(low_b, start, tile, 1)
        summed = summed + opening[pl.ds(start + 2, tile)].reshape(tile * pitch, ch).astype(F32)
        for shift in range(4):
            moved = summed if shift == 0 else roll_up(summed, shift)
            low_res[shift, pl.ds(start, tile)] = moved.astype(BF16).reshape(shape)[:, :narrow]

    blank_ends(low_res, 4, 2, 2)

    def tap(p, q):
        return up_w_ref[3 * p + q].astype(F32)

    groups = (((0,), (1, 2)), ((0, 1), (2,)))
    for a in range(2):
        for b in range(2):
            for p in range(2):
                for q in range(2):
                    summed = None
                    for pp in groups[a][p]:
                        for qq in groups[b][q]:
                            term = tap(pp, qq)
                            summed = term if summed is None else summed + term
                    base = (2 * p + q) * ch
                    phase_w[a, pl.ds(base, ch), pl.ds(b * ch, ch)] = summed.astype(BF16)

    total = rows + 2
    tile = tile_of(total, narrow)

    @pl.loop(0, total // tile)
    def _(step):
        start = step * tile
        shape = (tile, narrow, ch)
        for a in range(2):

            def up_conv(left, low_n, high_n):
                parts = []
                for p in range(2):
                    for q in range(2):
                        part = low_res[left + q, pl.ds(start + a + p, tile)]
                        parts.append(part.reshape(tile * narrow, ch))
                return jnp.dot(
                    jnp.concatenate(parts, axis=1),
                    phase_w[a, :, low_n:high_n],
                    preferred_element_type=F32,
                )

            def keep(slot, summed, kept):
                rounded = summed.astype(BF16)
                if kept is not None:
                    field[kept, pl.ds(start, tile), a] = rounded.reshape(shape)
                active = activate(rounded.astype(F32), high_gain_ref[0:1])
                high_a[slot, pl.ds(start, tile), a] = active.astype(BF16).reshape(shape)

            both = up_conv(1, 0, 2 * ch)
            keep(0, both[:, :ch], 0)
            keep(2, both[:, ch:], None)
            keep(1, up_conv(0, 0, ch), None)
            keep(3, up_conv(2, ch, 2 * ch), 1)

    blank_ends(high_a, 4, 1, 1)

    def high_conv(source, slots, start, tile, which):
        parts = []
        views = [
            source[s, pl.ds(start, tile // 2 + 1)].reshape(tile + 2, narrow, ch) for s in slots
        ]
        for p in range(3):
            for q in range(3):
                parts.append(views[q][p : p + tile].reshape(tile * narrow, ch))
        return jnp.dot(
            jnp.concatenate(parts, axis=1), high_w_ref[which], preferred_element_type=F32
        )

    total = 2 * rows + 2
    tile = tile_of(total, narrow, True)

    @pl.loop(0, total // tile)
    def _(step):
        half = tile // 2
        start = step * half
        shape = (half, 2, narrow, ch)
        gain = high_gain_ref[1:2]
        even = activate(high_conv(high_a, (2, 0, 3), start, tile, 0), gain)
        high_b[0, pl.ds(start, half)] = even.astype(BF16).reshape(shape)
        high_b[1, pl.ds(start, half)] = roll_up(even, 1).astype(BF16).reshape(shape)
        odd = activate(high_conv(high_a, (1, 2, 0), start, tile, 0), gain)
        high_b[2, pl.ds(start, half)] = odd.astype(BF16).reshape(shape)
        high_b[3, pl.ds(start, half)] = roll_up(odd, 1).astype(BF16).reshape(shape)

    last = high_b.shape[1] - 1

    @pl.when(at_top)
    def _():
        for k in range(4):
            high_b[k, 0, 0] = jnp.zeros((narrow, ch), BF16)

    @pl.when(at_bottom)
    def _():
        for k in range(4):
            high_b[k, last, 1] = jnp.zeros((narrow, ch), BF16)

    total = 2 * rows
    tile = tile_of(total, narrow, True)

    @pl.loop(0, total // tile)
    def _(step):
        half = tile // 2
        start = step * half
        shape = (tile, narrow, ch)
        for phase, slots in ((0, (2, 0, 3)), (1, (0, 3, 1))):
            summed = high_conv(high_b, slots, start, tile, 1)
            kept = field[phase, pl.ds(start + 1, half)].reshape(tile * narrow, ch)
            summed = (summed + kept.astype(F32)).reshape(tile * narrow, ch)
            summed = summed.reshape(shape)
            for lane in range(0, ch, 128):
                weave[lane // 128, :, pl.ds(phase, narrow, stride=2), :] = summed[
                    :, :, lane : lane + 128
                ]
        for lane in range(0, ch, 128):
            out_ref[pl.ds(2 * start, tile), :, lane : lane + 128] = weave[
                lane // 128, :, : 2 * cols, :
            ].astype(BF16)


def decode(band, patches, first, low_w, up_w, high_w, low_gain, high_gain, rows, cols, bands):
    pitch = patches.shape[1]
    ch = first.shape[1]
    narrow = round_up(cols + 1, 16)
    dims = (rows, cols, pitch, narrow, bands)
    vmem = pl.BlockSpec(memory_space=pltpu.VMEM)
    last_tile = tile_of(2 * rows, narrow, True)
    return pl.pallas_call(
        functools.partial(decoder_kernel, dims),
        out_shape=jax.ShapeDtypeStruct((2 * rows, 2 * cols, ch), BF16),
        in_specs=[pl.BlockSpec(memory_space=pltpu.SMEM)] + [vmem] * 7,
        out_specs=vmem,
        scratch_shapes=[
            pltpu.VMEM((rows + 8, pitch, ch), BF16),
            pltpu.VMEM((3, rows + 8, pitch, ch), BF16),
            pltpu.VMEM((3, rows + 6, pitch, ch), BF16),
            pltpu.VMEM((4, rows + 4, narrow, ch), BF16),
            pltpu.VMEM((2, 4 * ch, 2 * ch), BF16),
            pltpu.VMEM((2, rows + 2, 2, narrow, ch), BF16),
            pltpu.VMEM((4, rows + 2, 2, narrow, ch), BF16),
            pltpu.VMEM((4, rows + 1, 2, narrow, ch), BF16),
            pltpu.VMEM((ch // 128, last_tile, 2 * narrow, 128), F32),
        ],
        compiler_params=pltpu.CompilerParams(vmem_limit_bytes=56 * 1024 * 1024),
    )(band, patches, first, low_w, up_w, high_w, low_gain, high_gain)


def shards(
    denoised_tokens,
    sequence_row_index,
    latent_frame_cache,
    cache_slot_order,
    temporal_taps_weight,
    input_weight,
    latent_conv_weights,
    upsampled_weight,
    upper_conv_weights,
    latent_norm_gains,
    upper_norm_gains,
):
    sectors = lax.axis_size("lon")
    bands = lax.axis_size("band")
    rows = latent_frame_cache.shape[1]
    channels = temporal_taps_weight.shape[1]
    cols = latent_frame_cache.shape[2] // channels
    ch = input_weight.shape[2]
    edge = HALO * channels
    own = cols * channels
    wide = own + 2 * edge

    tokens = denoised_tokens.reshape(denoised_tokens.shape[1], denoised_tokens.shape[2])
    ring = jnp.concatenate([tokens[:, -edge:], tokens, tokens[:, :edge]], axis=1)
    windows = jnp.stack([ring[:, k * own : k * own + wide] for k in range(sectors)])
    arrived = lax.all_to_all(windows, "lon", split_axis=0, concat_axis=0, tiled=True)
    arrived = arrived.reshape(rows, wide)
    places = sequence_row_index[0][:, None] == jnp.arange(rows)[None, :]
    latent = jnp.dot(places.astype(BF16), arrived, preferred_element_type=F32).astype(BF16)

    frames = jnp.stack(
        [latent_frame_cache[cache_slot_order[0]], latent_frame_cache[cache_slot_order[1]]]
    )
    east = [(k, (k + 1) % sectors) for k in range(sectors)]
    west = [(target, source) for source, target in east]
    before = lax.ppermute(frames[:, :, -edge:], "lon", east)
    after = lax.ppermute(frames[:, :, :edge], "lon", west)
    frames = jnp.concatenate([before, frames, after], axis=2)
    stacked = jnp.concatenate([latent[None], frames], axis=0)
    south = [(k, k + 1) for k in range(bands - 1)]
    north = [(target, source) for source, target in south]
    above = lax.ppermute(stacked[:, -HALO:], "band", south)
    below = lax.ppermute(stacked[:, :HALO], "band", north)
    stacked = jnp.concatenate([above, stacked, below], axis=1)

    tall = rows + 2 * HALO
    span = cols + 2 * HALO
    cells = stacked.reshape(3, tall, span, channels).transpose(1, 2, 0, 3)
    cells = cells.reshape(tall * span, 3 * channels)
    taps = temporal_taps_weight.reshape(3 * channels, channels)
    temporal = jnp.dot(cells, taps, preferred_element_type=F32).astype(BF16)
    temporal = temporal.reshape(tall, span, channels)
    pitch = round_up(span, 16)
    temporal = jnp.pad(temporal, ((0, 0), (0, pitch + 2 - span), (0, 0)))
    patches = jnp.concatenate(
        [temporal[p : p + rows + 8, q : q + pitch] for p in range(3) for q in range(3)], axis=2
    )
    band = lax.axis_index("band").reshape(1).astype(jnp.int32)
    return decode(
        band,
        patches,
        input_weight.reshape(9 * channels, ch),
        latent_conv_weights.reshape(2, 9 * ch, ch),
        upsampled_weight,
        upper_conv_weights.reshape(2, 9 * ch, ch),
        latent_norm_gains,
        upper_norm_gains,
        rows,
        cols,
        bands,
    )


def solution(mesh):
    in_specs = (
        P("band", "lon", None),
        P("band", None),
        P(None, "band", "lon"),
        P(),
        P(),
        P(),
        P(),
        P(),
        P(),
        P(),
        P(),
    )
    out_specs = P("band", "lon", None)
    return jax.shard_map(shards, mesh=mesh, in_specs=in_specs, out_specs=out_specs, check_vma=False)
```

time: 270 us -> 66.5 us (0.25); the launches traced: 265 us -> 65.7 us
  local copies, waits for them, and re-layouts: 88.8 us -> 18.2 us
  matrix products: 68.6 us -> 1.04 us
  starting transfers between devices: 76.4 us -> 17.6 us
  Pallas kernels: 0 us -> 18.8 us
  other arithmetic: 17.7 us -> 2.99 us
  waiting for transfers between devices: 8.69 us -> 3.4 us
    dot_general x57 -> x2, matrix products: 68.6 us -> 1.04 us  [the longest x1 0.85 us: shards(): jnp.dot(places.astype(BF16), arrived, preferred_element_type=F32)]
    ppermute x24 -> x4, starting transfers between devices: 70 us -> 11.2 us  [the longest x1 5.11 us: shards(): above = lax.ppermute(stacked[:, -HALO:], 'band', south)]
    reshape x55 -> x4, local copies, waits for them, and re-layouts: 48.5 us -> 1.1 us  [the longest x2 0.6 us: shards(): temporal = temporal.reshape(tall, span, channels)]
    slice x33 -> x3, local copies, waits for them, and re-layouts: 23.4 us -> 2.58 us  [the longest x1 1.31 us: shards(): cache_slot_order[0]]
    pallas_call x0 -> x1, Pallas kernels: none -> 18.8 us  [decode(): pl.pallas_call(functools.partial(decoder_kernel, dims), out_shape=jax.Sha...]
    concatenate x14 -> x1, other arithmetic: 11.4 us -> 0.11 us  [shards(): stacked = jnp.concatenate([above, stacked, below], axis=1)]
    convert_element_type x6 -> x0, other arithmetic: 5.47 us -> none  [the longest x4 3.43 us: activate(): return jax.nn.silu(scaled).astype(jnp.bfloat16)]
    ppermute x24 -> x4, waiting for transfers between devices: 8.68 us -> 3.4 us  [the longest x1 3.2 us: shards(): below = lax.ppermute(stacked[:, :HALO], 'band', north)]
  transfers between devices with their start and end apart: 25 -> 5, of which waited for: 4 -> 2; matrix products, arithmetic and copies ran while one was open for 13% -> 5% of each run, Pallas kernels for 0% -> 0%
where the time goes in v1:
time: 66.5 us; the launch traced here: 65.7 us
  Pallas kernels  18.8 us (28%)
  local copies, waits for them, and re-layouts  18.2 us (27%)
  starting transfers between devices  17.6 us (26%)
  between operations  3.68 us (6%)
  waiting for transfers between devices  3.4 us (5%)
  other arithmetic  2.99 us (4%)
  matrix products  1.04 us (2%)
    pallas_call x1, Pallas kernels, decode(): pl.pallas_call(functools.partial(decoder_kernel, dims), out_shape=jax.Sha...  18.8 us
    unnamed x8, local copies, waits for them, and re-layouts  8.07 us
    all_to_all x1, starting transfers between devices, shards(): lax.all_to_all(windows, 'lon', split_axis=0, concat_axis=0, tiled=True)  6.38 us
    ppermute x1, starting transfers between devices, shards(): above = lax.ppermute(stacked[:, -HALO:], 'band', south)  5.11 us
    ppermute x1, waiting for transfers between devices, shards(): below = lax.ppermute(stacked[:, :HALO], 'band', north)  3.2 us
    ppermute x1, starting transfers between devices, shards(): after = lax.ppermute(frames[:, :, :edge], 'lon', west)  2.76 us
    pallas_call x1, local copies, waits for them, and re-layouts, decode(): pl.pallas_call(functools.partial(decoder_kernel, dims), out_shape=jax.Sha...  2.71 us
    concatenate x1, local copies, waits for them, and re-layouts, shards(): jnp.concatenate([temporal[p:p + rows + 8, q:q + pitch] for p in range(3)...  2.28 us
  transfers between devices with their start and end apart: 5, of which 2 were waited for; matrix products, arithmetic and copies ran while one was open for 5% of the time, Pallas kernels for 0%

profile of v1, /device:TPU:1, one launch (start us, length us, event | category | flops | bytes accessed | tf_op | source)
XLA Modules:
  0.0 65.7 jit_solution(7300203494616696619)
XLA Ops:
  0.0 0.0 copy-start
  0.0 0.8 %fusion.5 = (bf16[4,80]{1,0:T(4,128)(2,1)S(1)}, bf16[4,80]{1,0:T(4,128)(2,1)S(1)}) fusion(bf16[4,1920]{1,0:T(4,128)(2,1)} %bitcast.57), kind=kLoop, calls=%fused_computation.44 | loop fusion | bytes 2560 | tf_op jit(solution)/shard_map/slice | solution.py:307
  0.8 1.4 %constant_dynamic-update-slice_fusion.7 = bf16[8,4,400]{2,1,0:T(4,128)(2,1)} fusion(bf16[4,1920]{1,0:T(4,128)(2,1)} %bitcast.58, bf16[4,80]{1,0:T(4,128)(2,1)S(1)} %get-tuple-element.21), kind=kLoop, calls=%fused_computation.27 | loop fusion | flops 6399 | bytes 20096
  2.1 1.4 %constant_dynamic-update-slice_fusion.6 = bf16[8,4,400]{2,1,0:T(4,128)(2,1)} fusion(bf16[8,4,400]{2,1,0:T(4,128)(2,1)} %constant_dynamic-update-slice_fusion.7, bf16[4,1920]{1,0:T(4,128)(2,1)} %bitcast.59), kind=kLoop, calls=%fused_computation.26 | loop fusion | bytes 8192
  3.5 1.4 %constant_dynamic-update-slice_fusion.5 = bf16[8,4,400]{2,1,0:T(4,128)(2,1)} fusion(bf16[8,4,400]{2,1,0:T(4,128)(2,1)} %constant_dynamic-update-slice_fusion.6, bf16[4,1920]{1,0:T(4,128)(2,1)} %bitcast.60), kind=kLoop, calls=%fused_computation.25 | loop fusion | bytes 8192
  4.9 1.3 %constant_dynamic-update-slice_fusion.4 = bf16[8,4,400]{2,1,0:T(4,128)(2,1)} fusion(bf16[8,4,400]{2,1,0:T(4,128)(2,1)} %constant_dynamic-update-slice_fusion.5, bf16[4,1920]{1,0:T(4,128)(2,1)} %bitcast.61), kind=kLoop, calls=%fused_computation.24 | loop fusion | bytes 8192
  6.1 1.4 %constant_dynamic-update-slice_fusion.3 = bf16[8,4,400]{2,1,0:T(4,128)(2,1)} fusion(bf16[8,4,400]{2,1,0:T(4,128)(2,1)} %constant_dynamic-update-slice_fusion.4, bf16[4,1920]{1,0:T(4,128)(2,1)} %bitcast.62), kind=kLoop, calls=%fused_computation.23 | loop fusion | bytes 8192
  7.5 1.4 %constant_dynamic-update-slice_fusion.2 = bf16[8,4,400]{2,1,0:T(4,128)(2,1)} fusion(bf16[8,4,400]{2,1,0:T(4,128)(2,1)} %constant_dynamic-update-slice_fusion.3, bf16[4,1920]{1,0:T(4,128)(2,1)} %bitcast.63), kind=kLoop, calls=%fused_computation.22 | loop fusion | bytes 8192
  8.8 1.4 %constant_dynamic-update-slice_fusion.1 = bf16[8,4,400]{2,1,0:T(4,128)(2,1)} fusion(bf16[8,4,400]{2,1,0:T(4,128)(2,1)} %constant_dynamic-update-slice_fusion.2, bf16[4,1920]{1,0:T(4,128)(2,1)} %bitcast.64), kind=kLoop, calls=%fused_computation.21 | loop fusion | bytes 8192
  10.2 1.4 %constant_dynamic-update-slice_fusion = bf16[8,4,400]{2,1,0:T(4,128)(2,1)} fusion(bf16[8,4,400]{2,1,0:T(4,128)(2,1)} %constant_dynamic-update-slice_fusion.1, bf16[4,80]{1,0:T(4,128)(2,1)S(1)} %get-tuple-element.20, bf16[4,1920]{1,0:T(4,128)(2,1)} %bitcast.65), kind=kLoop, calls=%fused_computation.20 | loop fusion | flops 6400 | bytes 20096 | tf_op jit(solution)/shard_map/stack | solution.py:308
  11.6 6.4 %all-to-all-start = ((bf16[8,4,400]{2,1,0:T(4,128)(2,1)}), bf16[8,4,400]{2,1,0:T(4,128)(2,1)S(1)}, u32[]{:S(2)}, u32[]{:S(2)}) async-start(bf16[8,4,400]{2,1,0:T(4,128)(2,1)} %constant_dynamic-update-slice_fusion), calls=%async_computation | async-start | bytes 65536 | tf_op jit(solution)/shard_map/all_to_all | solution.py:309
  17.9 1.3 %fusion.6 = (s32[1]{0:T(128)}, s32[1]{0:T(128)}) fusion(s32[4]{0:T(128)} %param.14), kind=kLoop, calls=%fused_computation.45 | loop fusion | bytes 16 | tf_op jit(solution)/shard_map/slice | solution.py:315
  22.9 0.7 %constant_dynamic-slice_fusion.1 = (bf16[1,32,240]{2,1,0:T(8,128)(2,1)S(1)}, bf16[1,32,240]{2,1,0:T(8,128)(2,1)S(1)}) fusion(bf16[4,32,240]{2,1,0:T(8,128)(2,1)} %param.13, s32[]{:T(128)S(6)} %select_n.6, s32[]{:T(128)S(6)} %select_n.7), kind=kLoop, calls=%fused_computation.43 | loop fusion | bytes 61448 | tf_op jit(solution)/shard_map/dynamic_slice | solution.py:315
  23.6 0.1 fusion.1
  23.7 1.5 %collective-permute-start = (bf16[2,32,80]{2,1,0:T(8,128)(2,1)S(1)}, bf16[2,32,80]{2,1,0:T(8,128)(2,1)S(1)}, u32[]{:S(2)}, u32[]{:S(2)}) collective-permute-start(bf16[2,32,80]{2,1,0:T(8,128)(2,1)S(1)} %get-tuple-element.18), channel_id=1, source_target_pairs={{0,4},{4,8},{8,12},{12,16},{16,20},{20,24},{24,28},{28,0},{1,5},{5... | collective-permute-start | bytes 30728 | tf_op jit(solution)/shard_map/ppermute | solution.py:319
  25.1 2.8 %collective-permute-start.1 = (bf16[2,32,80]{2,1,0:T(8,128)(2,1)S(1)}, bf16[2,32,80]{2,1,0:T(8,128)(2,1)S(1)}, u32[]{:S(2)}, u32[]{:S(2)}) collective-permute-start(bf16[2,32,80]{2,1,0:T(8,128)(2,1)S(1)} %get-tuple-element.19), channel_id=1, source_target_pairs={{4,0},{8,4},{12,8},{16,12},{20,16},{24,20},{28,24},{0,28},{5,1},{9... | collective-permute-start | bytes 30728 | tf_op jit(solution)/shard_map/ppermute | solution.py:320
  27.9 0.0 all-to-all-done
  27.9 0.8 %fusion = bf16[1,32,400]{2,1,0:T(8,128)(2,1)S(1)} fusion(bf16[32,400]{1,0:T(8,128)(2,1)S(1)} %reshape.33, s32[32]{0:T(128)} %bitcast.67), kind=kOutput, calls=%fused_computation.2 | convolution fusion | flops 833024 | bytes 51328 | tf_op jit(solution)/shard_map/dot_general | solution.py:312
  28.8 0.2 collective-permute-done
  29.0 0.0 collective-permute-done.1
  29.0 0.1 pad_maximum_fusion.5
  29.1 5.1 %collective-permute-start.2 = (bf16[3,5,400]{2,1,0:T(8,128)(2,1)S(1)}, bf16[3,5,400]{2,1,0:T(8,128)(2,1)S(1)}, u32[]{:S(2)}, u32[]{:S(2)}) collective-permute-start(bf16[3,5,400]{2,1,0:T(8,128)(2,1)S(1)} %get-tuple-element.14), channel_id=1, source_target_pairs={{0,1},{1,2},{2,3},{4,5},{5,6},{6,7},{8,9},{9,10},{10,11},{12,13},{... | collective-permute-start | bytes 36008 | tf_op jit(solution)/shard_map/ppermute | solution.py:325
  34.2 1.9 %collective-permute-start.3 = (bf16[3,5,400]{2,1,0:T(8,128)(2,1)S(1)}, bf16[3,5,400]{2,1,0:T(8,128)(2,1)S(1)}, u32[]{:S(2)}, u32[]{:S(2)}) collective-permute-start(bf16[3,5,400]{2,1,0:T(8,128)(2,1)S(1)} %get-tuple-element.15), channel_id=1, source_target_pairs={{1,0},{2,1},{3,2},{5,4},{6,5},{7,6},{9,8},{10,9},{11,10},{13,12},{... | collective-permute-start | bytes 36008 | tf_op jit(solution)/shard_map/ppermute | solution.py:326
  36.1 0.0 collective-permute-done.2
  36.1 3.2 %collective-permute-done.3 = bf16[3,5,400]{2,1,0:T(8,128)(2,1)S(1)} collective-permute-done((bf16[3,5,400]{2,1,0:T(8,128)(2,1)S(1)}, bf16[3,5,400]{2,1,0:T(8,128)(2,1)S(1)}, u32[]{:S(2)}, u32[]{:S(2)}) %collective-permute-start.3) | collective-permute-done | bytes 12032 | tf_op jit(solution)/shard_map/ppermute | solution.py:326
  39.3 0.1 pad_maximum_fusion
  39.4 0.3 copy.20
  39.7 0.5 copy.21
  40.2 0.5 reshape.35
  40.7 0.0 copy-done
  40.7 0.2 convolution_convert_fusion
  40.9 0.2 reshape.37
  41.1 0.4 copy.22
  41.5 0.5 pad_slice_fusion
  42.0 2.3 %concatenate.24.patches_ref = bf16[40,32,144]{2,1,0:T(8,128)(2,1)} concatenate(bf16[40,32,16]{2,1,0:T(8,128)(2,1)S(1)} %get-tuple-element.13, bf16[40,32,16]{2,1,0:T(8,128)(2,1)S(1)} %get-tuple-element.6, bf16[40,32,16]{2,1,0:T(8,128)(2,1)S(1)} %get-tuple-element.7, bf16[40,32,16]{2,1,0:T(8,128)(2,1)S(1)} %get-tuple-element.8, bf16[40,32,16]{2,1,0:T(8,128)(2,1)S(1)} %get-tuple-element.9, ...), dimensions={2} | concatenate | bytes 737280 | tf_op jit(solution)/shard_map/concatenate | solution.py:338
  44.3 18.8 %shard_map.109 = bf16[64,30,256]{2,1,0:T(8,128)(2,1)} custom-call(s32[1]{0:T(128)} %bitcast.band_ref, bf16[40,32,144]{2,1,0:T(8,128)(2,1)} %concatenate.24.patches_ref, bf16[144,256]{1,0:T(8,128)(2,1)} %bitcast.66, bf16[2,2304,256]{2,1,0:T(8,128)(2,1)} %bitcast.54, bf16[9,256,256]{2,1,0:T(8,128)(2,1)} %up_w_ref.1, bf16[2,2304,256]{2,1,0:T(8,128)(2,1)} %bitcast.55, ...), custom_call_target="tpu_custom_call" | custom-call | tf_op jit(solution)/shard_map/pallas_call | solution.py:263
  63.0 2.7 %copy.23 = bf16[64,30,256]{2,0,1:T(8,128)(2,1)} copy(bf16[64,30,256]{2,1,0:T(8,128)(2,1)} %shard_map.109) | data formatting | bytes 1966080 | tf_op jit(solution)/shard_map/pallas_call | solution.py:263
  (1 shorter events, 0.0 us)
Async XLA Ops:
  0.0 40.7 %copy-start = (bf16[3,16,16]{2,1,0:T(8,128)(2,1)S(1)}, bf16[3,16,16]{2,1,0:T(8,128)(2,1)}, u32[]{:S(2)}) copy-start(bf16[3,16,16]{2,1,0:T(8,128)(2,1)} %param.15) | copy-start | bytes 4612
  11.6 16.3 %all-to-all-start = ((bf16[8,4,400]{2,1,0:T(4,128)(2,1)}), bf16[8,4,400]{2,1,0:T(4,128)(2,1)S(1)}, u32[]{:S(2)}, u32[]{:S(2)}) async-start(bf16[8,4,400]{2,1,0:T(4,128)(2,1)} %constant_dynamic-update-slice_fusion), calls=%async_computation | async-start | bytes 65536 | tf_op jit(solution)/shard_map/all_to_all | solution.py:309
  23.7 5.3 %collective-permute-start = (bf16[2,32,80]{2,1,0:T(8,128)(2,1)S(1)}, bf16[2,32,80]{2,1,0:T(8,128)(2,1)S(1)}, u32[]{:S(2)}, u32[]{:S(2)}) collective-permute-start(bf16[2,32,80]{2,1,0:T(8,128)(2,1)S(1)} %get-tuple-element.18), channel_id=1, source_target_pairs={{0,4},{4,8},{8,12},{12,16},{16,20},{20,24},{24,28},{28,0},{1,5},{5... | collective-permute-start | bytes 30728 | tf_op jit(solution)/shard_map/ppermute | solution.py:319
  25.1 3.8 %collective-permute-start.1 = (bf16[2,32,80]{2,1,0:T(8,128)(2,1)S(1)}, bf16[2,32,80]{2,1,0:T(8,128)(2,1)S(1)}, u32[]{:S(2)}, u32[]{:S(2)}) collective-permute-start(bf16[2,32,80]{2,1,0:T(8,128)(2,1)S(1)} %get-tuple-element.19), channel_id=1, source_target_pairs={{4,0},{8,4},{12,8},{16,12},{20,16},{24,20},{28,24},{0,28},{5,1},{9... | collective-permute-start | bytes 30728 | tf_op jit(solution)/shard_map/ppermute | solution.py:320
  29.1 7.1 %collective-permute-start.2 = (bf16[3,5,400]{2,1,0:T(8,128)(2,1)S(1)}, bf16[3,5,400]{2,1,0:T(8,128)(2,1)S(1)}, u32[]{:S(2)}, u32[]{:S(2)}) collective-permute-start(bf16[3,5,400]{2,1,0:T(8,128)(2,1)S(1)} %get-tuple-element.14), channel_id=1, source_target_pairs={{0,1},{1,2},{2,3},{4,5},{5,6},{6,7},{8,9},{9,10},{10,11},{12,13},{... | collective-permute-start | bytes 36008 | tf_op jit(solution)/shard_map/ppermute | solution.py:325
  34.2 5.1 %collective-permute-start.3 = (bf16[3,5,400]{2,1,0:T(8,128)(2,1)S(1)}, bf16[3,5,400]{2,1,0:T(8,128)(2,1)S(1)}, u32[]{:S(2)}, u32[]{:S(2)}) collective-permute-start(bf16[3,5,400]{2,1,0:T(8,128)(2,1)S(1)} %get-tuple-element.15), channel_id=1, source_target_pairs={{1,0},{2,1},{3,2},{5,4},{6,5},{7,6},{9,8},{10,9},{11,10},{13,12},{... | collective-permute-start | bytes 36008 | tf_op jit(solution)/shard_map/ppermute | solution.py:326

commit v2 on v1

--- a/solution.py
+++ b/solution.py
@@ -8,6 +8,9 @@
 from jax.sharding import PartitionSpec as P
 
 HALO = 5
+LANES = 128
+ROWS = 16
+MESH = pl.DeviceIdType.MESH
 F32 = jnp.float32
 BF16 = jnp.bfloat16
 
@@ -244,12 +247,14 @@
             summed = (summed + kept.astype(F32)).reshape(tile * narrow, ch)
             summed = summed.reshape(shape)
             for lane in range(0, ch, 128):
-                weave[lane // 128, :, pl.ds(phase, narrow, stride=2), :] = summed[
-                    :, :, lane : lane + 128
-                ]
+                for t in range(tile):
+                    spots = pl.ds(phase * total + 2 * start + t, narrow, stride=2 * total)
+                    weave[lane // 128, spots, :] = summed[t, :, lane : lane + 128]
+
+    for col in range(2 * cols):
         for lane in range(0, ch, 128):
-            out_ref[pl.ds(2 * start, tile), :, lane : lane + 128] = weave[
-                lane // 128, :, : 2 * cols, :
+            out_ref[col, :, lane : lane + 128] = weave[
+                lane // 128, pl.ds(col * total, total), :
             ].astype(BF16)
 
 
@@ -259,10 +264,9 @@
     narrow = round_up(cols + 1, 16)
     dims = (rows, cols, pitch, narrow, bands)
     vmem = pl.BlockSpec(memory_space=pltpu.VMEM)
-    last_tile = tile_of(2 * rows, narrow, True)
     return pl.pallas_call(
         functools.partial(decoder_kernel, dims),
-        out_shape=jax.ShapeDtypeStruct((2 * rows, 2 * cols, ch), BF16),
+        out_shape=jax.ShapeDtypeStruct((2 * cols, 2 * rows, ch), BF16),
         in_specs=[pl.BlockSpec(memory_space=pltpu.SMEM)] + [vmem] * 7,
         out_specs=vmem,
         scratch_shapes=[
@@ -274,10 +278,176 @@
             pltpu.VMEM((2, rows + 2, 2, narrow, ch), BF16),
             pltpu.VMEM((4, rows + 2, 2, narrow, ch), BF16),
             pltpu.VMEM((4, rows + 1, 2, narrow, ch), BF16),
-            pltpu.VMEM((ch // 128, last_tile, 2 * narrow, 128), F32),
+            pltpu.VMEM((ch // 128, 2 * narrow * 2 * rows, 128), F32),
         ],
         compiler_params=pltpu.CompilerParams(vmem_limit_bytes=56 * 1024 * 1024),
     )(band, patches, first, low_w, up_w, high_w, low_gain, high_gain)
+
+
+def halo_kernel(
+    dims, tokens_ref, places_ref, cache_ref, order_ref, arrived, places, frames, ring, *sems
+):
+    edge, sectors, bands, window = dims
+    token_send, token_recv, place_send, place_recv, frame_send, frame_recv, own_sem = sems
+    lon = lax.axis_index("lon")
+    band = lax.axis_index("band")
+    length = tokens_ref.shape[1]
+    own = cache_ref.shape[2]
+    rows = cache_ref.shape[1]
+    broad = round_up(own, LANES)
+
+    def sector(step):
+        return lax.rem(lon + step + sectors, sectors)
+
+    def inside(step):
+        return jnp.logical_and(band + step >= 0, band + step < bands)
+
+    def to(across, down):
+        return {"lon": sector(across), "band": band + down}
+
+    barrier = pltpu.get_barrier_semaphore()
+    for down in (0, 1, -1):
+
+        @pl.when(inside(down))
+        def _():
+            for across in range(sectors):
+                if across or down:
+                    pl.semaphore_signal(
+                        barrier, inc=1, device_id=to(across, down), device_id_type=MESH
+                    )
+
+    ring[:, :LANES] = tokens_ref[:, length - LANES :]
+    ring[:, LANES : LANES + length] = tokens_ref[...]
+    ring[:, LANES + length :] = tokens_ref[:, : 2 * LANES]
+    frames[:, ROWS : ROWS + rows, LANES : LANES + broad] = jnp.zeros(
+        (2, rows, broad), frames.dtype
+    )
+    for k in range(2):
+        frames[k, ROWS : ROWS + rows, LANES : LANES + own] = cache_ref[order_ref[k]]
+    places[1] = places_ref[...]
+    for slot, step, spot in ((0, -1, 0), (2, 1, ROWS + rows)):
+
+        @pl.when(jnp.logical_not(inside(step)))
+        def _():
+            arrived[slot] = jnp.zeros(arrived.shape[1:], arrived.dtype)
+            places[slot] = jnp.zeros(places.shape[1:], places.dtype)
+            frames[:, spot : spot + ROWS] = jnp.zeros(
+                (2, ROWS, frames.shape[2]), frames.dtype
+            )
+
+    neighbours = jnp.where(inside(-1), 1, 0) + jnp.where(inside(1), 1, 0) + 1
+    pl.semaphore_wait(barrier, neighbours * sectors - 1)
+
+    def token_copy(across, down, source):
+        start = (sector(across) * own + LANES - edge) // LANES * LANES
+        return pltpu.make_async_remote_copy(
+            src_ref=ring.at[:, pl.ds(pl.multiple_of(start, LANES), window)],
+            dst_ref=arrived.at[1 - down, source],
+            send_sem=token_send.at[1 - down, across],
+            recv_sem=token_recv.at[1 - down, across],
+            device_id=to(across, down),
+            device_id_type=MESH,
+        )
+
+    def place_copy(down):
+        return pltpu.make_async_remote_copy(
+            src_ref=places_ref,
+            dst_ref=places.at[1 - down],
+            send_sem=place_send.at[1 - down],
+            recv_sem=place_recv.at[1 - down],
+            device_id=to(0, down),
+            device_id_type=MESH,
+        )
+
+    def frame_copy(across, down):
+        tall = {0: (ROWS, ROWS, rows), 1: (rows, 0, ROWS), -1: (ROWS, ROWS + rows, ROWS)}[down]
+        inner = LANES + (own - edge) // LANES * LANES
+        flat = {
+            0: (LANES, LANES, broad),
+            1: (inner, 0, LANES),
+            -1: (LANES, LANES + broad, LANES),
+        }[across]
+        return pltpu.make_async_remote_copy(
+            src_ref=frames.at[:, pl.ds(tall[0], tall[2]), pl.ds(flat[0], flat[2])],
+            dst_ref=frames.at[:, pl.ds(tall[1], tall[2]), pl.ds(flat[1], flat[2])],
+            send_sem=frame_send.at[down + 1, across + 1],
+            recv_sem=frame_recv.at[down + 1, across + 1],
+            device_id=to(across, down),
+            device_id_type=MESH,
+        )
+
+    mine = (lon * own + LANES - edge) // LANES * LANES
+    stay = pltpu.make_async_copy(
+        ring.at[:, pl.ds(pl.multiple_of(mine, LANES), window)], arrived.at[1, lon], own_sem
+    )
+    for down in (1, -1, 0):
+
+        @pl.when(inside(down))
+        def _():
+            for across in range(sectors):
+                if across or down:
+                    token_copy(across, down, lon).start()
+            for across in (-1, 0, 1):
+                if across or down:
+                    frame_copy(across, down).start()
+            if down:
+                place_copy(down).start()
+
+    stay.start()
+    for down in (0, 1, -1):
+
+        @pl.when(inside(down))
+        def _():
+            for across in range(sectors):
+                if across or down:
+                    token_copy(across, down, lon).wait_send()
+            for across in (-1, 0, 1):
+                if across or down:
+                    frame_copy(across, down).wait_send()
+            if down:
+                place_copy(down).wait_send()
+
+        @pl.when(inside(-down))
+        def _():
+            for across in range(sectors):
+                if across or down:
+                    token_copy(across, down, sector(-across)).wait_recv()
+            for across in (-1, 0, 1):
+                if across or down:
+                    frame_copy(across, down).wait_recv()
+            if down:
+                place_copy(down).wait_recv()
+
+    stay.wait()
+
+
+def gather_halos(tokens, places, cache, order, edge, sectors, bands):
+    own = cache.shape[2]
+    rows = cache.shape[1]
+    window = round_up(own + 2 * edge + LANES - edge // HALO, LANES)
+    vmem = pl.BlockSpec(memory_space=pltpu.VMEM)
+    dma = pltpu.SemaphoreType.DMA
+    return pl.pallas_call(
+        functools.partial(halo_kernel, (edge, sectors, bands, window)),
+        out_shape=[
+            jax.ShapeDtypeStruct((3, sectors, tokens.shape[0], window), BF16),
+            jax.ShapeDtypeStruct((3,) + places.shape, places.dtype),
+            jax.ShapeDtypeStruct((2, rows + 2 * ROWS, round_up(own, LANES) + 2 * LANES), BF16),
+        ],
+        in_specs=[vmem, vmem, vmem, pl.BlockSpec(memory_space=pltpu.SMEM)],
+        out_specs=[vmem] * 3,
+        scratch_shapes=[
+            pltpu.VMEM((tokens.shape[0], tokens.shape[1] + 3 * LANES), BF16),
+            dma((3, sectors)),
+            dma((3, sectors)),
+            dma((3,)),
+            dma((3,)),
+            dma((3, 3)),
+            dma((3, 3)),
+            dma,
+        ],
+        compiler_params=pltpu.CompilerParams(collective_id=0, has_side_effects=True),
+    )(tokens, places, cache, order)
 
 
 def shards(
@@ -303,28 +473,36 @@
     own = cols * channels
     wide = own + 2 * edge
 
-    tokens = denoised_tokens.reshape(denoised_tokens.shape[1], denoised_tokens.shape[2])
-    ring = jnp.concatenate([tokens[:, -edge:], tokens, tokens[:, :edge]], axis=1)
-    windows = jnp.stack([ring[:, k * own : k * own + wide] for k in range(sectors)])
-    arrived = lax.all_to_all(windows, "lon", split_axis=0, concat_axis=0, tiled=True)
-    arrived = arrived.reshape(rows, wide)
-    places = sequence_row_index[0][:, None] == jnp.arange(rows)[None, :]
-    latent = jnp.dot(places.astype(BF16), arrived, preferred_element_type=F32).astype(BF16)
-
-    frames = jnp.stack(
-        [latent_frame_cache[cache_slot_order[0]], latent_frame_cache[cache_slot_order[1]]]
-    )
-    east = [(k, (k + 1) % sectors) for k in range(sectors)]
-    west = [(target, source) for source, target in east]
-    before = lax.ppermute(frames[:, :, -edge:], "lon", east)
-    after = lax.ppermute(frames[:, :, :edge], "lon", west)
-    frames = jnp.concatenate([before, frames, after], axis=2)
+    arrived, places, frames = gather_halos(
+        denoised_tokens.reshape(denoised_tokens.shape[1:]),
+        sequence_row_index,
+        latent_frame_cache,
+        cache_slot_order,
+        edge,
+        sectors,
+        bands,
+    )
+    order = jnp.concatenate(
+        [places[0, 0, -HALO:], places[1, 0] + rows, places[2, 0, :HALO] + 2 * rows]
+    )
+    chosen = (order[:, None] == jnp.arange(3 * rows)[None, :]).astype(BF16)
+    arrived = arrived.reshape(3 * rows, arrived.shape[3])
+    latent = jnp.dot(chosen, arrived, preferred_element_type=F32).astype(BF16)
+    skew = lax.rem(lax.axis_index("lon") * own + LANES - edge, LANES)
+    latent = lax.dynamic_slice_in_dim(latent, skew, wide, 1)
+    inner = (own - edge) // LANES * LANES
+    left = own - edge - inner
+    broad = round_up(own, LANES)
+    frames = frames[:, ROWS - HALO : ROWS + rows + HALO]
+    frames = jnp.concatenate(
+        [
+            frames[:, :, left : left + edge],
+            frames[:, :, LANES : LANES + own],
+            frames[:, :, LANES + broad : LANES + broad + edge],
+        ],
+        axis=2,
+    )
     stacked = jnp.concatenate([latent[None], frames], axis=0)
-    south = [(k, k + 1) for k in range(bands - 1)]
-    north = [(target, source) for source, target in south]
-    above = lax.ppermute(stacked[:, -HALO:], "band", south)
-    below = lax.ppermute(stacked[:, :HALO], "band", north)
-    stacked = jnp.concatenate([above, stacked, below], axis=1)
 
     tall = rows + 2 * HALO
     span = cols + 2 * HALO
@@ -339,7 +517,7 @@
         [temporal[p : p + rows + 8, q : q + pitch] for p in range(3) for q in range(3)], axis=2
     )
     band = lax.axis_index("band").reshape(1).astype(jnp.int32)
-    return decode(
+    decoded = decode(
         band,
         patches,
         input_weight.reshape(9 * channels, ch),
@@ -352,6 +530,7 @@
         cols,
         bands,
     )
+    return decoded.transpose(1, 0, 2)
 
 
 def solution(mesh):

time: 66.5 us -> 43.4 us (0.65)
  starting transfers between devices: 17.6 us -> 0 us
  Pallas kernels: 18.8 us -> 32.7 us
  local copies, waits for them, and re-layouts: 18.2 us -> 8.06 us
  between operations: 3.68 us -> 0.08 us
  waiting for transfers between devices: 3.4 us -> 0 us
  other arithmetic: 2.99 us -> 1.59 us
    pallas_call x0 -> x1, Pallas kernels: none -> 12.1 us  [gather_halos(): pl.pallas_call(functools.partial(halo_kernel, (edge, sectors, bands, wind...]
    ppermute x4 -> x0, starting transfers between devices: 11.2 us -> none  [the longest x1 5.11 us: shards(): above = lax.ppermute(stacked[:, -HALO:], 'band', south)]
    unnamed x8 -> x2, local copies, waits for them, and re-layouts: 8.07 us -> 0.71 us
    all_to_all x1 -> x0, starting transfers between devices: 6.38 us -> none  [shards(): lax.all_to_all(windows, 'lon', split_axis=0, concat_axis=0, tiled=True)]
    ppermute x4 -> x0, waiting for transfers between devices: 3.4 us -> none  [the longest x1 3.2 us: shards(): below = lax.ppermute(stacked[:, :HALO], 'band', north)]
    pallas_call x1 -> x0, local copies, waits for them, and re-layouts: 2.71 us -> none  [decode(): pl.pallas_call(functools.partial(decoder_kernel, dims), out_shape=jax.Sha...]
    pallas_call x1, Pallas kernels: 18.8 us -> 20.6 us  [decode(): pl.pallas_call(functools.partial(decoder_kernel, dims), out_shape=jax.Sha...]
    another operation x2 -> x0, other arithmetic: 1.43 us -> none  [the longest x1 1.35 us: shards(): jnp.stack([ring[:, k * own:k * own + wide] for k in range(sectors)])]
  transfers between devices with their start and end apart: 5 -> 0, of which waited for: 2 -> 0; matrix products, arithmetic and copies ran while one was open for 5% -> 0% of each run, Pallas kernels for 0% -> 0%
where the time goes in v2:
time: 43.4 us; the launch traced here: 42.8 us
  Pallas kernels  32.7 us (75%)
  local copies, waits for them, and re-layouts  8.06 us (19%)
  other arithmetic  1.59 us (4%)
    pallas_call x1, Pallas kernels, decode(): pl.pallas_call(functools.partial(decoder_kernel, dims), out_shape=jax.Sha...  20.6 us
    pallas_call x1, Pallas kernels, gather_halos(): pl.pallas_call(functools.partial(halo_kernel, (edge, sectors, bands, wind...  12.1 us
    concatenate x1, local copies, waits for them, and re-layouts, shards(): jnp.concatenate([temporal[p:p + rows + 8, q:q + pitch] for p in range(3)...  2.27 us
    reshape x1, local copies, waits for them, and re-layouts, shards(): arrived = arrived.reshape(3 * rows, arrived.shape[3])  0.92 us

profile of v2, /device:TPU:1, one launch (start us, length us, event | category | flops | bytes accessed | tf_op | source)
XLA Modules:
  0.0 42.8 jit_solution(9828179583631540556)
XLA Ops:
  0.0 0.0 copy-start
  0.0 0.7 %copy-done = bf16[3,16,16]{2,1,0:T(8,128)(2,1)S(1)} copy-done((bf16[3,16,16]{2,1,0:T(8,128)(2,1)S(1)}, bf16[3,16,16]{2,1,0:T(8,128)(2,1)}, u32[]{:S(2)}) %copy-start) | copy-done | bytes 1560
  0.7 12.1 %shard_map.109 = (bf16[3,8,4,512]{3,2,1,0:T(4,128)(2,1)}, s32[3,1,32]{2,1,0:T(1,128)}, bf16[2,64,512]{2,1,0:T(8,128)(2,1)}) custom-call(bf16[4,1920]{1,0:T(4,128)(2,1)} %bitcast.30, s32[1,32]{1,0:T(1,128)} %places_ref.1, bf16[4,32,240]{2,1,0:T(8,128)(2,1)} %cache_ref.1, s32[4]{0:T(128)} %order_ref.1), custom_call_target="tpu_custom_call" | custom-call | tf_op jit(solution)/shard_map/pallas_call | solution.py:430
  12.8 0.9 %reshape.38 = bf16[96,512]{1,0:T(8,128)(2,1)S(1)} reshape(bf16[3,8,4,512]{3,2,1,0:T(4,128)(2,1)} %get-tuple-element.9) | data formatting | bytes 196608 | tf_op jit(solution)/shard_map/reshape | solution.py:489
  13.7 0.6 %add_bitcast_fusion.1 = s32[32]{0:T(128)S(1)} fusion(s32[3,1,32]{2,1,0:T(1,128)} %get-tuple-element.8), kind=kLoop, calls=%fused_computation.18 | loop fusion | flops 32 | bytes 256 | tf_op jit(solution)/shard_map/add | solution.py:486
  14.3 0.7 %slice_bitcast_fusion = (s32[5]{0:T(128)S(1)}, s32[5]{0:T(128)S(1)}) fusion(s32[3,1,32]{2,1,0:T(1,128)} %get-tuple-element.8), kind=kLoop, calls=%fused_computation.19 | loop fusion | flops 5 | bytes 80 | tf_op jit(solution)/shard_map/squeeze | solution.py:486
  15.1 0.1 pad_add_fusion
  15.2 0.2 fusion
  15.4 0.1 dynamic-slice_convert_fusion
  15.5 0.8 %slice.53 = bf16[2,42,240]{2,1,0:T(8,128)(2,1)S(1)} slice(bf16[2,64,512]{2,1,0:T(8,128)(2,1)} %get-tuple-element.10), slice={[0:2], [11:53], [128:368]} | slice | bytes 80640 | tf_op jit(solution)/shard_map/slice | solution.py:500
  16.3 0.9 %fusion.2 = (bf16[2,42,80]{2,1,0:T(8,128)(2,1)S(1)}, bf16[2,42,80]{2,1,0:T(8,128)(2,1)S(1)}) fusion(bf16[2,64,512]{2,1,0:T(8,128)(2,1)} %get-tuple-element.10), kind=kLoop, calls=%fused_computation.20 | loop fusion | bytes 53760 | tf_op jit(solution)/shard_map/slice | solution.py:499
  17.2 0.1 pad_maximum_fusion
  17.3 0.1 copy.13
  17.4 0.2 copy.14
  17.6 0.1 maximum_bitcast_fusion
  17.7 0.5 %copy.15 = bf16[42,25,3,16]{1,0,3,2:T(8,128)(2,1)S(1)} copy(bf16[42,25,3,16]{0,3,1,2:T(8,128)(2,1)S(1)} %maximum_bitcast_fusion) | data formatting | bytes 201600 | tf_op jit(solution)/shard_map/transpose | solution.py:509
  18.2 0.5 %reshape.39 = bf16[1050,48]{0,1:T(8,128)(2,1)S(1)} reshape(bf16[42,25,3,16]{1,0,3,2:T(8,128)(2,1)S(1)} %copy.15) | data formatting | bytes 201600 | tf_op jit(solution)/shard_map/reshape | solution.py:510
  18.6 0.2 convolution_convert_fusion
  18.8 0.2 reshape.41
  19.1 0.4 copy.16
  19.5 0.5 %pad_slice_fusion = (bf16[40,32,16]{2,1,0:T(8,128)(2,1)S(1)}, bf16[40,32,16]{2,1,0:T(8,128)(2,1)S(1)}, bf16[40,32,16]{2,1,0:T(8,128)(2,1)S(1)}, bf16[40,32,16]{2...) fusion(bf16[42,25,16]{2,1,0:T(8,128)(2,1)S(1)} %copy.16), kind=kLoop, calls=%fused_computation.1 | loop fusion | bytes 402240 | tf_op jit(solution)/shard_map/slice | solution.py:517
  19.9 2.3 %concatenate.22.patches_ref = bf16[40,32,144]{2,1,0:T(8,128)(2,1)} concatenate(bf16[40,32,16]{2,1,0:T(8,128)(2,1)S(1)} %get-tuple-element.19, bf16[40,32,16]{2,1,0:T(8,128)(2,1)S(1)} %get-tuple-element.12, bf16[40,32,16]{2,1,0:T(8,128)(2,1)S(1)} %get-tuple-element.13, bf16[40,32,16]{2,1,0:T(8,128)(2,1)S(1)} %get-tuple-element.14, bf16[40,32,16]{2,1,0:T(8,128)(2,1)S(1)} %get-tuple-element.15, ...), dimensions={2} | concatenate | bytes 737280 | tf_op jit(solution)/shard_map/concatenate | solution.py:516
  22.2 20.6 %shard_map.110 = bf16[30,64,256]{2,1,0:T(8,128)(2,1)} custom-call(s32[1]{0:T(128)} %bitcast.band_ref, bf16[40,32,144]{2,1,0:T(8,128)(2,1)} %concatenate.22.patches_ref, bf16[144,256]{1,0:T(8,128)(2,1)} %bitcast.29, bf16[2,2304,256]{2,1,0:T(8,128)(2,1)} %bitcast.25, bf16[9,256,256]{2,1,0:T(8,128)(2,1)} %up_w_ref.1, bf16[2,2304,256]{2,1,0:T(8,128)(2,1)} %bitcast.26, ...), custom_call_target="tpu_custom_call" | custom-call | tf_op jit(solution)/shard_map/pallas_call | solution.py:267
Async XLA Ops:
  0.0 0.7 %copy-start = (bf16[3,16,16]{2,1,0:T(8,128)(2,1)S(1)}, bf16[3,16,16]{2,1,0:T(8,128)(2,1)}, u32[]{:S(2)}) copy-start(bf16[3,16,16]{2,1,0:T(8,128)(2,1)} %param.15) | copy-start | bytes 4612

commit v3 on v2

--- a/solution.py
+++ b/solution.py
@@ -39,15 +39,27 @@
 
 def decoder_kernel(
     dims,
-    band_ref,
-    patches_ref,
+    spot_ref,
+    arrived_ref,
+    places_ref,
+    frames_ref,
+    taps_ref,
     first_ref,
+    low_hbm,
+    up_hbm,
+    high_hbm,
+    low_gain_ref,
+    high_gain_ref,
+    out_ref,
     low_w_ref,
     up_w_ref,
     high_w_ref,
-    low_gain_ref,
-    high_gain_ref,
-    out_ref,
+    weight_sems,
+    sorted_rows,
+    rim_rows,
+    strip,
+    first_w,
+    fresh,
     opening,
     low_a,
     low_b,
@@ -60,7 +72,7 @@
 ):
     rows, cols, pitch, narrow, bands = dims
     ch = out_ref.shape[-1]
-    band = band_ref[0]
+    band = spot_ref[0]
     at_top = band == 0
     at_bottom = band == bands - 1
 
@@ -84,14 +96,115 @@
             for k in range(copies):
                 blank(ref, k, pl.ds(total - bottom, bottom))
 
+    loads = [
+        pltpu.make_async_copy(source, target, weight_sems.at[k])
+        for k, (source, target) in enumerate(
+            (
+                (low_hbm.at[0], low_w_ref.at[0]),
+                (low_hbm.at[1], low_w_ref.at[1]),
+                (up_hbm, up_w_ref),
+                (high_hbm.at[0], high_w_ref.at[0]),
+                (high_hbm.at[1], high_w_ref.at[1]),
+            )
+        )
+    ]
+    for load in loads:
+        load.start()
+
+    window = arrived_ref.shape[3]
+    held = arrived_ref.shape[2]
+    channels = taps_ref.shape[1]
+    edge = HALO * channels
+    own = cols * channels
+    broad = round_up(own, LANES)
+    tall = round_up(rows + 2 * HALO, 16)
+    for slot in range(3):
+        for source in range(arrived_ref.shape[1]):
+            at = slot * rows + source * held
+            strip[at : at + held] = arrived_ref[slot, source].astype(F32)
+    for slot in range(3):
+        spots = jnp.broadcast_to(places_ref[slot], (rows, rows))
+        hits = spots == lax.broadcasted_iota(jnp.int32, (rows, rows), 0)
+        chosen = jnp.where(hits, 1.0, 0.0).T.astype(BF16)
+        band_rows = strip[slot * rows : (slot + 1) * rows].astype(BF16)
+        sorted_rows[slot * rows : (slot + 1) * rows] = jnp.dot(
+            chosen, band_rows, preferred_element_type=F32
+        )
+    latent = sorted_rows[rows - HALO : rows - HALO + tall]
+    sources = [pltpu.roll(latent, window - spot_ref[1], 1)]
+
+    lanes = frames_ref.shape[2]
+    inner = (own - edge) // LANES * LANES
+    left = own - edge - inner
+    lane = lax.broadcasted_iota(jnp.int32, (tall, lanes), 1)
+    for k in range(2):
+        rim_rows[...] = frames_ref[k].astype(F32)
+        mosaic = rim_rows[ROWS - HALO : ROWS - HALO + tall]
+        west = pltpu.roll(mosaic, lanes - left, 1) if left else mosaic
+        middle = pltpu.roll(mosaic, lanes - (LANES - edge), 1)
+        east = pltpu.roll(mosaic, lanes - (LANES + broad - edge - own), 1)
+        sources.append(jnp.where(lane < edge, west, jnp.where(lane < edge + own, middle, east)))
+
+    spread = lax.broadcasted_iota(jnp.int32, (LANES, channels), 0) % channels
+    spread = spread == lax.broadcasted_iota(jnp.int32, (LANES, channels), 1)
+    spread = jnp.where(spread, 1.0, 0.0).astype(BF16)
+    gather = lax.broadcasted_iota(jnp.int32, (channels, LANES), 1) % channels
+    gather = gather == lax.broadcasted_iota(jnp.int32, (channels, LANES), 0)
+    gather = jnp.where(gather, 1.0, 0.0).astype(BF16)
+    same = lax.broadcasted_iota(jnp.int32, (LANES, LANES), 0) // channels
+    same = same == lax.broadcasted_iota(jnp.int32, (LANES, LANES), 1) // channels
+    blocks = []
+    for k in range(3):
+        deep = jnp.dot(spread, taps_ref[k], preferred_element_type=F32).astype(BF16)
+        deep = jnp.dot(deep, gather, preferred_element_type=F32)
+        blocks.append(jnp.where(same, deep, 0.0).astype(BF16))
+    blocks = jnp.concatenate(blocks, axis=0)
+    span = round_up((cols + 2 * HALO) * channels, LANES)
+    strip[tall : tall + 8, :span] = jnp.zeros((8, span), F32)
+    for tile in range(0, span, LANES):
+        mixed = jnp.concatenate([source[:, tile : tile + LANES] for source in sources], axis=1)
+        temporal = jnp.dot(mixed.astype(BF16), blocks, preferred_element_type=F32)
+        strip[:tall, tile : tile + LANES] = temporal.astype(BF16).astype(F32)
+
+    deep = 3 * channels
+    first_w[...] = jnp.zeros(first_w.shape, BF16)
+    for p in range(3):
+        first_w[p * LANES : p * LANES + deep] = first_ref[p * deep : (p + 1) * deep]
+    shifted = [strip[p : p + tall, :span] for p in range(3)]
+    group = 8
+    for begin in range(0, cols + 8, group):
+        stack = []
+        columns = range(begin, min(begin + group, cols + 8))
+        for col in columns:
+            base = col * channels // LANES * LANES
+            skew = col * channels - base
+            pieces = []
+            for p in range(3):
+                if skew + deep <= LANES:
+                    piece = shifted[p][:, base : base + LANES]
+                    piece = pltpu.roll(piece, LANES - skew, 1) if skew else piece
+                else:
+                    piece = shifted[p][:, base : base + 2 * LANES]
+                    piece = pltpu.roll(piece, 2 * LANES - skew, 1)[:, :LANES]
+                pieces.append(piece.astype(BF16))
+            stack.append(jnp.concatenate(pieces, axis=1))
+        summed = jnp.dot(
+            jnp.concatenate(stack, axis=0), first_w[...], preferred_element_type=F32
+        )
+        for k, col in enumerate(columns):
+            for half in range(0, ch, LANES):
+                fresh[half // LANES, pl.ds(col, rows + 8, stride=pitch), :] = summed[
+                    k * tall : k * tall + rows + 8, half : half + LANES
+                ]
+
     total = rows + 8
     tile = tile_of(total, pitch)
 
     @pl.loop(0, total // tile)
     def _(step):
         start = step * tile
-        part = patches_ref[pl.ds(start, tile)].reshape(tile * pitch, -1)
-        summed = jnp.dot(part, first_ref[...], preferred_element_type=F32)
+        flat = pl.ds(pl.multiple_of(start * pitch, 16), tile * pitch)
+        summed = jnp.concatenate([fresh[half, flat, :] for half in range(ch // LANES)], axis=1)
         summed = summed.astype(BF16).astype(F32)
         shape = (tile, pitch, ch)
         opening[pl.ds(start, tile)] = roll_up(summed, 2).astype(BF16).reshape(shape)
@@ -100,6 +213,7 @@
         low_a[1, pl.ds(start, tile)] = roll_up(active, 1).astype(BF16).reshape(shape)
         low_a[2, pl.ds(start, tile)] = roll_up(active, 2).astype(BF16).reshape(shape)
 
+    loads[0].wait()
     blank_ends(low_a, 3, 4, 4)
 
     def low_conv(source, start, tile, which):
@@ -125,6 +239,7 @@
         low_b[2, pl.ds(start, tile)] = roll_up(active, 2).astype(BF16).reshape(shape)
 
     blank_ends(low_b, 3, 3, 3)
+    loads[1].wait()
 
     total = rows + 4
     tile = tile_of(total, pitch)
@@ -140,6 +255,8 @@
             low_res[shift, pl.ds(start, tile)] = moved.astype(BF16).reshape(shape)[:, :narrow]
 
     blank_ends(low_res, 4, 2, 2)
+
+    loads[2].wait()
 
     def tap(p, q):
         return up_w_ref[3 * p + q].astype(F32)
@@ -192,6 +309,7 @@
             keep(3, up_conv(2, ch, 2 * ch), 1)
 
     blank_ends(high_a, 4, 1, 1)
+    loads[3].wait()
 
     def high_conv(source, slots, start, tile, which):
         parts = []
@@ -232,6 +350,8 @@
     def _():
         for k in range(4):
             high_b[k, last, 1] = jnp.zeros((narrow, ch), BF16)
+
+    loads[4].wait()
 
     total = 2 * rows
     tile = tile_of(total, narrow, True)
@@ -258,18 +378,28 @@
             ].astype(BF16)
 
 
-def decode(band, patches, first, low_w, up_w, high_w, low_gain, high_gain, rows, cols, bands):
-    pitch = patches.shape[1]
+def decode(spot, arrived, places, frames, taps, first, low_w, up_w, high_w, gains, dims):
+    rows, cols, pitch, narrow, bands = dims
     ch = first.shape[1]
-    narrow = round_up(cols + 1, 16)
-    dims = (rows, cols, pitch, narrow, bands)
+    window = arrived.shape[3]
+    tall = round_up(rows + 2 * HALO, 16)
     vmem = pl.BlockSpec(memory_space=pltpu.VMEM)
+    hbm = pl.BlockSpec(memory_space=pl.ANY)
     return pl.pallas_call(
         functools.partial(decoder_kernel, dims),
         out_shape=jax.ShapeDtypeStruct((2 * cols, 2 * rows, ch), BF16),
-        in_specs=[pl.BlockSpec(memory_space=pltpu.SMEM)] + [vmem] * 7,
+        in_specs=[pl.BlockSpec(memory_space=pltpu.SMEM)] + [vmem] * 5 + [hbm] * 3 + [vmem] * 2,
         out_specs=vmem,
         scratch_shapes=[
+            pltpu.VMEM(low_w.shape, BF16),
+            pltpu.VMEM(up_w.shape, BF16),
+            pltpu.VMEM(high_w.shape, BF16),
+            pltpu.SemaphoreType.DMA((5,)),
+            pltpu.VMEM((3 * rows + tall, window), F32),
+            pltpu.VMEM((rows + 2 * ROWS, frames.shape[2]), F32),
+            pltpu.VMEM((max(3 * rows, tall + 8), window), F32),
+            pltpu.VMEM((3 * LANES, ch), BF16),
+            pltpu.VMEM((ch // LANES, (rows + 8) * pitch, LANES), F32),
             pltpu.VMEM((rows + 8, pitch, ch), BF16),
             pltpu.VMEM((3, rows + 8, pitch, ch), BF16),
             pltpu.VMEM((3, rows + 6, pitch, ch), BF16),
@@ -278,10 +408,10 @@
             pltpu.VMEM((2, rows + 2, 2, narrow, ch), BF16),
             pltpu.VMEM((4, rows + 2, 2, narrow, ch), BF16),
             pltpu.VMEM((4, rows + 1, 2, narrow, ch), BF16),
-            pltpu.VMEM((ch // 128, 2 * narrow * 2 * rows, 128), F32),
+            pltpu.VMEM((ch // LANES, 2 * narrow * 2 * rows, LANES), F32),
         ],
         compiler_params=pltpu.CompilerParams(vmem_limit_bytes=56 * 1024 * 1024),
-    )(band, patches, first, low_w, up_w, high_w, low_gain, high_gain)
+    )(spot, arrived, places, frames, taps, first, low_w, up_w, high_w, *gains)
 
 
 def halo_kernel(
@@ -471,7 +601,6 @@
     ch = input_weight.shape[2]
     edge = HALO * channels
     own = cols * channels
-    wide = own + 2 * edge
 
     arrived, places, frames = gather_halos(
         denoised_tokens.reshape(denoised_tokens.shape[1:]),
@@ -482,53 +611,23 @@
         sectors,
         bands,
     )
-    order = jnp.concatenate(
-        [places[0, 0, -HALO:], places[1, 0] + rows, places[2, 0, :HALO] + 2 * rows]
-    )
-    chosen = (order[:, None] == jnp.arange(3 * rows)[None, :]).astype(BF16)
-    arrived = arrived.reshape(3 * rows, arrived.shape[3])
-    latent = jnp.dot(chosen, arrived, preferred_element_type=F32).astype(BF16)
-    skew = lax.rem(lax.axis_index("lon") * own + LANES - edge, LANES)
-    latent = lax.dynamic_slice_in_dim(latent, skew, wide, 1)
-    inner = (own - edge) // LANES * LANES
-    left = own - edge - inner
-    broad = round_up(own, LANES)
-    frames = frames[:, ROWS - HALO : ROWS + rows + HALO]
-    frames = jnp.concatenate(
-        [
-            frames[:, :, left : left + edge],
-            frames[:, :, LANES : LANES + own],
-            frames[:, :, LANES + broad : LANES + broad + edge],
-        ],
-        axis=2,
-    )
-    stacked = jnp.concatenate([latent[None], frames], axis=0)
-
-    tall = rows + 2 * HALO
-    span = cols + 2 * HALO
-    cells = stacked.reshape(3, tall, span, channels).transpose(1, 2, 0, 3)
-    cells = cells.reshape(tall * span, 3 * channels)
-    taps = temporal_taps_weight.reshape(3 * channels, channels)
-    temporal = jnp.dot(cells, taps, preferred_element_type=F32).astype(BF16)
-    temporal = temporal.reshape(tall, span, channels)
-    pitch = round_up(span, 16)
-    temporal = jnp.pad(temporal, ((0, 0), (0, pitch + 2 - span), (0, 0)))
-    patches = jnp.concatenate(
-        [temporal[p : p + rows + 8, q : q + pitch] for p in range(3) for q in range(3)], axis=2
-    )
-    band = lax.axis_index("band").reshape(1).astype(jnp.int32)
+    lon = lax.axis_index("lon")
+    skew = lax.rem(lon * own + LANES - edge, LANES)
+    spot = jnp.stack([lax.axis_index("band"), skew]).astype(jnp.int32)
+    pitch = round_up(cols + 8, 16)
+    narrow = round_up(cols + 1, 16)
     decoded = decode(
-        band,
-        patches,
+        spot,
+        arrived,
+        places,
+        frames,
+        temporal_taps_weight,
         input_weight.reshape(9 * channels, ch),
         latent_conv_weights.reshape(2, 9 * ch, ch),
         upsampled_weight,
         upper_conv_weights.reshape(2, 9 * ch, ch),
-        latent_norm_gains,
-        upper_norm_gains,
-        rows,
-        cols,
-        bands,
+        (latent_norm_gains, upper_norm_gains),
+        (rows, cols, pitch, narrow, bands),
     )
     return decoded.transpose(1, 0, 2)
 

time: 43.4 us -> 33.3 us (0.77)
  local copies, waits for them, and re-layouts: 8.06 us -> 0 us
  other arithmetic: 1.59 us -> 0.65 us
  Pallas kernels: 32.7 us -> 32.2 us
    concatenate x2 -> x0, local copies, waits for them, and re-layouts: 2.46 us -> none  [the longest x1 2.27 us: shards(): jnp.concatenate([temporal[p:p + rows + 8, q:q + pitch] for p in range(3)...]
    slice x3 -> x0, local copies, waits for them, and re-layouts: 2.18 us -> none  [the longest x1 0.85 us: shards(): frames[:, :, left:left + edge]]
    reshape x4 -> x0, local copies, waits for them, and re-layouts: 2 us -> none  [the longest x1 0.92 us: shards(): arrived = arrived.reshape(3 * rows, arrived.shape[3])]
    squeeze x1 -> x0, other arithmetic: 0.75 us -> none  [shards(): places[0, 0, -HALO:]]
    unnamed x2 -> x0, local copies, waits for them, and re-layouts: 0.71 us -> none
    another operation x0 -> x1, other arithmetic: none -> 0.65 us  [shards(): spot = jnp.stack([lax.axis_index('band'), skew]).astype(jnp.int32)]
    add x1 -> x0, other arithmetic: 0.6 us -> none  [shards(): places[1, 0] + rows]
    transpose x1 -> x0, local copies, waits for them, and re-layouts: 0.48 us -> none  [shards(): cells = stacked.reshape(3, tall, span, channels).transpose(1, 2, 0, 3)]
where the time goes in v3:
time: 33.3 us; the launch traced here: 32.9 us
  Pallas kernels  32.2 us (97%)
  other arithmetic  0.65 us (2%)
    pallas_call x1, Pallas kernels, decode(): pl.pallas_call(functools.partial(decoder_kernel, dims), out_shape=jax.Sha...  20.1 us
    pallas_call x1, Pallas kernels, gather_halos(): pl.pallas_call(functools.partial(halo_kernel, (edge, sectors, bands, wind...  12.1 us

profile of v3, /device:TPU:1, one launch (start us, length us, event | category | flops | bytes accessed | tf_op | source)
XLA Modules:
  0.0 32.9 jit_solution(4732642078887000116)
XLA Ops:
  0.0 0.6 %pad_add_fusion.spot_ref = s32[2]{0:T(128)} fusion(s32[1]{0:T(128)} %bitcast.1, s32[1]{0:T(128)} %bitcast), kind=kLoop, calls=%fused_computation | loop fusion | flops 2 | bytes 16 | tf_op jit(solution)/shard_map/stack | solution.py:616
  0.6 12.1 %shard_map.109 = (bf16[3,8,4,512]{3,2,1,0:T(4,128)(2,1)}, s32[3,1,32]{2,1,0:T(1,128)}, bf16[2,64,512]{2,1,0:T(8,128)(2,1)}) custom-call(bf16[4,1920]{1,0:T(4,128)(2,1)} %bitcast.10, s32[1,32]{1,0:T(1,128)} %places_ref.1, bf16[4,32,240]{2,1,0:T(8,128)(2,1)} %cache_ref.1, s32[4]{0:T(128)} %order_ref.1), custom_call_target="tpu_custom_call" | custom-call | tf_op jit(solution)/shard_map/pallas_call | solution.py:560
  12.8 20.1 %shard_map.110 = bf16[30,64,256]{2,1,0:T(8,128)(2,1)} custom-call(s32[2]{0:T(128)} %pad_add_fusion.spot_ref, bf16[3,8,4,512]{3,2,1,0:T(4,128)(2,1)} %get-tuple-element.8.arrived_ref, s32[3,1,32]{2,1,0:T(1,128)} %get-tuple-element.9.places_ref, bf16[2,64,512]{2,1,0:T(8,128)(2,1)} %get-tuple-element.10.frames_ref, bf16[3,16,16]{2,1,0:T(8,128)(2,1)} %taps_ref.1, ...), custom_call_target="tpu_custom_call" | custom-call | tf_op jit(solution)/shard_map/pallas_call | solution.py:388

commit v4 on v3

--- a/solution.py
+++ b/solution.py
@@ -39,7 +39,6 @@
 
 def decoder_kernel(
     dims,
-    spot_ref,
     arrived_ref,
     places_ref,
     frames_ref,
@@ -72,7 +71,7 @@
 ):
     rows, cols, pitch, narrow, bands = dims
     ch = out_ref.shape[-1]
-    band = spot_ref[0]
+    band = lax.axis_index("band")
     at_top = band == 0
     at_bottom = band == bands - 1
 
@@ -131,7 +130,8 @@
             chosen, band_rows, preferred_element_type=F32
         )
     latent = sorted_rows[rows - HALO : rows - HALO + tall]
-    sources = [pltpu.roll(latent, window - spot_ref[1], 1)]
+    skew = lax.rem(lax.axis_index("lon") * own + LANES - edge, LANES)
+    sources = [pltpu.roll(latent, window - skew, 1)]
 
     lanes = frames_ref.shape[2]
     inner = (own - edge) // LANES * LANES
@@ -200,7 +200,7 @@
     total = rows + 8
     tile = tile_of(total, pitch)
 
-    @pl.loop(0, total // tile)
+    @pl.loop(0, total // tile, unroll=total // tile)
     def _(step):
         start = step * tile
         flat = pl.ds(pl.multiple_of(start * pitch, 16), tile * pitch)
@@ -229,7 +229,7 @@
     total = rows + 6
     tile = tile_of(total, pitch)
 
-    @pl.loop(0, total // tile)
+    @pl.loop(0, total // tile, unroll=total // tile)
     def _(step):
         start = step * tile
         shape = (tile, pitch, ch)
@@ -244,7 +244,7 @@
     total = rows + 4
     tile = tile_of(total, pitch)
 
-    @pl.loop(0, total // tile)
+    @pl.loop(0, total // tile, unroll=total // tile)
     def _(step):
         start = step * tile
         shape = (tile, pitch, ch)
@@ -277,7 +277,7 @@
     total = rows + 2
     tile = tile_of(total, narrow)
 
-    @pl.loop(0, total // tile)
+    @pl.loop(0, total // tile, unroll=total // tile)
     def _(step):
         start = step * tile
         shape = (tile, narrow, ch)
@@ -326,7 +326,7 @@
     total = 2 * rows + 2
     tile = tile_of(total, narrow, True)
 
-    @pl.loop(0, total // tile)
+    @pl.loop(0, total // tile, unroll=total // tile)
     def _(step):
         half = tile // 2
         start = step * half
@@ -356,7 +356,7 @@
     total = 2 * rows
     tile = tile_of(total, narrow, True)
 
-    @pl.loop(0, total // tile)
+    @pl.loop(0, total // tile, unroll=total // tile)
     def _(step):
         half = tile // 2
         start = step * half
@@ -378,7 +378,7 @@
             ].astype(BF16)
 
 
-def decode(spot, arrived, places, frames, taps, first, low_w, up_w, high_w, gains, dims):
+def decode(arrived, places, frames, taps, first, low_w, up_w, high_w, gains, dims):
     rows, cols, pitch, narrow, bands = dims
     ch = first.shape[1]
     window = arrived.shape[3]
@@ -388,7 +388,7 @@
     return pl.pallas_call(
         functools.partial(decoder_kernel, dims),
         out_shape=jax.ShapeDtypeStruct((2 * cols, 2 * rows, ch), BF16),
-        in_specs=[pl.BlockSpec(memory_space=pltpu.SMEM)] + [vmem] * 5 + [hbm] * 3 + [vmem] * 2,
+        in_specs=[vmem] * 5 + [hbm] * 3 + [vmem] * 2,
         out_specs=vmem,
         scratch_shapes=[
             pltpu.VMEM(low_w.shape, BF16),
@@ -411,7 +411,7 @@
             pltpu.VMEM((ch // LANES, 2 * narrow * 2 * rows, LANES), F32),
         ],
         compiler_params=pltpu.CompilerParams(vmem_limit_bytes=56 * 1024 * 1024),
-    )(spot, arrived, places, frames, taps, first, low_w, up_w, high_w, *gains)
+    )(arrived, places, frames, taps, first, low_w, up_w, high_w, *gains)
 
 
 def halo_kernel(
@@ -611,13 +611,9 @@
         sectors,
         bands,
     )
-    lon = lax.axis_index("lon")
-    skew = lax.rem(lon * own + LANES - edge, LANES)
-    spot = jnp.stack([lax.axis_index("band"), skew]).astype(jnp.int32)
     pitch = round_up(cols + 8, 16)
     narrow = round_up(cols + 1, 16)
     decoded = decode(
-        spot,
         arrived,
         places,
         frames,

time: 33.3 us -> 31.8 us (0.955)
  Pallas kernels: 32.2 us -> 31.2 us
  other arithmetic: 0.65 us -> 0 us
    pallas_call x1, Pallas kernels: 20.1 us -> 19.1 us  [decode(): pl.pallas_call(functools.partial(decoder_kernel, dims), out_shape=jax.Sha...]
    another operation x1 -> x0, other arithmetic: 0.65 us -> none  [shards(): spot = jnp.stack([lax.axis_index('band'), skew]).astype(jnp.int32)]
where the time goes in v4:
time: 31.8 us; the launch traced here: 31.4 us
  Pallas kernels  31.2 us (98%)
    pallas_call x1, Pallas kernels, decode(): pl.pallas_call(functools.partial(decoder_kernel, dims), out_shape=jax.Sha...  19.1 us
    pallas_call x1, Pallas kernels, gather_halos(): pl.pallas_call(functools.partial(halo_kernel, (edge, sectors, bands, wind...  12.1 us

profile of v4, /device:TPU:1, one launch (start us, length us, event | category | flops | bytes accessed | tf_op | source)
XLA Modules:
  0.0 31.4 jit_solution(17140389150287042481)
XLA Ops:
  0.0 12.1 %shard_map.109 = (bf16[3,8,4,512]{3,2,1,0:T(4,128)(2,1)}, s32[3,1,32]{2,1,0:T(1,128)}, bf16[2,64,512]{2,1,0:T(8,128)(2,1)}) custom-call(bf16[4,1920]{1,0:T(4,128)(2,1)} %bitcast.8, s32[1,32]{1,0:T(1,128)} %places_ref.1, bf16[4,32,240]{2,1,0:T(8,128)(2,1)} %cache_ref.1, s32[4]{0:T(128)} %order_ref.1), custom_call_target="tpu_custom_call" | custom-call | tf_op jit(solution)/shard_map/pallas_call | solution.py:560
  12.1 19.1 %shard_map.110 = bf16[30,64,256]{2,1,0:T(8,128)(2,1)} custom-call(bf16[3,8,4,512]{3,2,1,0:T(4,128)(2,1)} %get-tuple-element.8.arrived_ref, s32[3,1,32]{2,1,0:T(1,128)} %get-tuple-element.9.places_ref, bf16[2,64,512]{2,1,0:T(8,128)(2,1)} %get-tuple-element.10.frames_ref, bf16[3,16,16]{2,1,0:T(8,128)(2,1)} %taps_ref.1, bf16[144,256]{1,0:T(8,128)(2,1)} %bitcast.7, ...), custom_call_target="tpu_custom_call" | custom-call | tf_op jit(solution)/shard_map/pallas_call | solution.py:388
